TPU v7x, 256 devices: a whole 4x4x8 slice. The times are simulated.
256 devices in a mesh: wide: 32 (over x, z_hi, core), narrow: 8 (over y, z_lo).
Axes of the slice: x: 4, y: 4, z: 8 (z_hi: 4, z_lo: 2; z = z_hi * 2 + z_lo), core: 2. Of those that a mesh axis runs over, the one named last changes fastest.
Arguments:
- stash_values: int32 [256, 256, 512], P('wide', 'narrow'), may hold values from -127 to 127
- scale_exp: int32 [32, 32], P('wide', 'narrow'), may hold values from -8 to -6
- w_qkv: bfloat16 [512, 1536], P('wide'), may hold values from -0.25 to 0.25
- w_out: bfloat16 [512, 512], P('wide'), may hold values from -0.25 to 0.25
- w_reduce: bfloat16 [2048, 1024], P('wide'), may hold values from -0.125 to 0.125
- logit_scale: float32 [16], replicated, may hold values from 2 to 20
- bias_table: float32 [225, 16], replicated, may hold values from -6 to 6
- rel_index: int32 [64, 64], replicated, may hold values from 0 to 224
- norm_gain: float32 [512], replicated, may hold values from 0.1 to 1.9
- merge_gain: float32 [1024], replicated, may hold values from 0.1 to 1.9
- cotangent: bfloat16 [128, 128, 1024], P('wide', 'narrow'), may hold values from -6 to 6
Outputs:
- merged: bfloat16 [128, 128, 1024], P('wide', 'narrow')
- grad_input: bfloat16 [256, 256, 512], P('wide', 'narrow')
- grad_qkv: float32 [512, 1536], P('wide', 'narrow')
- grad_out: float32 [512, 512], P('wide', 'narrow')
- grad_reduce: float32 [2048, 1024], P('wide', 'narrow')
All inputs are finite; a program needn't handle non-finite values.
Results may differ from a plain program's by a relative error of at most 0.03.
Values may be sent and summed in bfloat16 or wider, within the bound.
A program may use at most 64 MiB of HBM per device.

v0:
```python
import math

import jax
import jax.numpy as jnp
from jax import lax
from jax.sharding import PartitionSpec as P

WIN = 8


def from_behind(block, axis, distance):
    devices = range(lax.axis_size(axis))
    route = [((i - distance) % len(devices), i) for i in devices]
    return lax.ppermute(block, axis, route)


def dequantize(stash_values, scale_exp):
    tile_rows, tile_cols, channels = stash_values.shape
    factor = jnp.exp2(scale_exp.astype(jnp.float32))
    blocks = stash_values.astype(jnp.float32).reshape(
        tile_rows // WIN, WIN, tile_cols // WIN, WIN, channels
    )
    scaled = blocks * factor[:, None, :, None, None]
    return scaled.reshape(tile_rows, tile_cols, channels).astype(jnp.bfloat16)


def to_windows(grid):
    tile_rows, tile_cols, channels = grid.shape
    blocks = grid.reshape(tile_rows // WIN, WIN, tile_cols // WIN, WIN, channels).transpose(
        0, 2, 1, 3, 4
    )
    return blocks.reshape(-1, WIN * WIN, channels)


def from_windows(windows, tile_rows, tile_cols):
    channels = windows.shape[-1]
    blocks = windows.reshape(tile_rows // WIN, tile_cols // WIN, WIN, WIN, channels).transpose(
        0, 2, 1, 3, 4
    )
    return blocks.reshape(tile_rows, tile_cols, channels)


def merge_tokens(grid):
    tile_rows, tile_cols, channels = grid.shape
    blocks = grid.reshape(tile_rows // 2, 2, tile_cols // 2, 2, channels).transpose(0, 2, 3, 1, 4)
    return blocks.reshape(tile_rows // 2, tile_cols // 2, 4 * channels)


def split_tokens(joined):
    half_rows, half_cols, wide_channels = joined.shape
    channels = wide_channels // 4
    blocks = joined.reshape(half_rows, half_cols, 2, 2, channels).transpose(0, 3, 1, 2, 4)
    return blocks.reshape(half_rows * 2, half_cols * 2, channels)


def layer_norm(values_in, gain):
    average = jnp.mean(values_in, -1, keepdims=True)
    centred = values_in - average
    variance = jnp.mean(centred * centred, -1, keepdims=True)
    return centred * lax.rsqrt(variance + 1e-05) * gain


def relative_bias(rel_index, bias_table):
    table_rows = bias_table.shape[0]
    onehot = (
        rel_index[:, :, None] == jnp.arange(table_rows, dtype=jnp.int32)[None, None, :]
    ).astype(jnp.float32)
    return jnp.einsum(
        "abr,rh->hab", onehot, 16.0 * jax.nn.sigmoid(bias_table), precision=lax.Precision.HIGHEST
    )


def shift_mask(row_first, col_first, tile_rows, tile_cols, total_rows, total_cols):
    half_win = WIN // 2
    grid_row = row_first + jnp.arange(tile_rows, dtype=jnp.int32)
    grid_col = col_first + jnp.arange(tile_cols, dtype=jnp.int32)
    row_label = (grid_row >= total_rows - WIN).astype(jnp.int32) + (
        grid_row >= total_rows - half_win
    ).astype(jnp.int32)
    col_label = (grid_col >= total_cols - WIN).astype(jnp.int32) + (
        grid_col >= total_cols - half_win
    ).astype(jnp.int32)
    labels = row_label[:, None] * 3 + col_label[None, :]
    win_labels = to_windows(labels[:, :, None])[:, :, 0]
    same = win_labels[:, :, None] == win_labels[:, None, :]
    return jnp.where(same, 0.0, -100.0).astype(jnp.float32)


def window_attention(qkv_windows, logit_scale, pos_bias, win_mask):
    heads = logit_scale.shape[0]
    count, tokens, triple = qkv_windows.shape
    head_size = triple // 3 // heads
    pieces = qkv_windows.astype(jnp.float32).reshape(count, tokens, 3, heads, head_size)
    queries = pieces[:, :, 0]
    key_rows = pieces[:, :, 1]
    val_rows = pieces[:, :, 2]
    query_norm = jnp.maximum(jnp.sqrt(jnp.sum(queries * queries, -1, keepdims=True)), 1e-12)
    key_norm = jnp.maximum(jnp.sqrt(jnp.sum(key_rows * key_rows, -1, keepdims=True)), 1e-12)
    cosines = jnp.einsum(
        "wihd,wjhd->whij",
        queries / query_norm,
        key_rows / key_norm,
        precision=lax.Precision.HIGHEST,
    )
    scores = cosines * logit_scale[None, :, None, None] + pos_bias[None] + win_mask[:, None]
    weights_exp = jnp.exp(scores)
    attn_probs = (weights_exp / jnp.sum(weights_exp, -1, keepdims=True)).astype(jnp.bfloat16)
    attended = jnp.einsum(
        "whij,wjhd->wihd", attn_probs.astype(jnp.float32), val_rows, precision=lax.Precision.HIGHEST
    )
    return attended.reshape(count, tokens, heads * head_size).astype(jnp.bfloat16)


def roll_ahead(tensor, amount):
    fresh_rows = from_behind(tensor[:amount], "wide", -1)
    row_moved = jnp.concatenate([tensor[amount:], fresh_rows], 0)
    fresh_cols = from_behind(row_moved[:, :amount], "narrow", -1)
    return jnp.concatenate([row_moved[:, amount:], fresh_cols], 1)


def roll_behind(tensor, amount):
    fresh_rows = from_behind(tensor[-amount:], "wide", 1)
    row_moved = jnp.concatenate([fresh_rows, tensor[:-amount]], 0)
    fresh_cols = from_behind(row_moved[:, -amount:], "narrow", 1)
    return jnp.concatenate([fresh_cols, row_moved[:, :-amount]], 1)


def on_device(
    stash_values,
    scale_exp,
    w_qkv,
    w_out,
    w_reduce,
    logit_scale,
    bias_table,
    rel_index,
    norm_gain,
    merge_gain,
    cotangent,
):
    tile_rows, tile_cols, width = stash_values.shape
    half_win = WIN // 2
    total_rows = tile_rows * lax.axis_size("wide")
    total_cols = tile_cols * lax.axis_size("narrow")
    inputs = dequantize(stash_values, scale_exp)
    gathered_qkv, gathered_out, gathered_reduce = (
        lax.all_gather(w_qkv, "wide", axis=0, tiled=True),
        lax.all_gather(w_out, "wide", axis=0, tiled=True),
        lax.all_gather(w_reduce, "wide", axis=0, tiled=True),
    )
    pos_bias = relative_bias(rel_index, bias_table)
    win_mask = shift_mask(
        lax.axis_index("wide") * tile_rows,
        lax.axis_index("narrow") * tile_cols,
        tile_rows,
        tile_cols,
        total_rows,
        total_cols,
    )
    rolled = roll_ahead(inputs, half_win)
    flat_rows = rolled.reshape(-1, width)
    qkv_rows = jnp.dot(flat_rows, gathered_qkv, preferred_element_type=jnp.float32).astype(
        jnp.bfloat16
    )

    def attend(windows_in):
        return window_attention(windows_in, logit_scale, pos_bias, win_mask)

    attended_win, attn_back = jax.vjp(
        attend, to_windows(qkv_rows.reshape(tile_rows, tile_cols, 3 * width))
    )
    attended = from_windows(attended_win, tile_rows, tile_cols).reshape(-1, width)
    projected = jnp.dot(attended, gathered_out, preferred_element_type=jnp.float32)

    def post_norm(values_in):
        return layer_norm(values_in, norm_gain)

    normed, norm_back = jax.vjp(post_norm, projected)
    rolled_out = (
        (flat_rows.astype(jnp.float32) + normed)
        .astype(jnp.bfloat16)
        .reshape(tile_rows, tile_cols, width)
    )
    merge_source = roll_behind(rolled_out, half_win)
    joined = merge_tokens(merge_source).reshape(-1, 4 * width)
    reduced = jnp.dot(joined, gathered_reduce, preferred_element_type=jnp.float32)

    def merge_norm(values_in):
        return layer_norm(values_in, merge_gain)

    merge_normed, merge_back = jax.vjp(merge_norm, reduced)
    merge_local = merge_normed.astype(jnp.bfloat16).reshape(
        tile_rows // 2, tile_cols // 2, 2 * width
    )
    grad_reduced = merge_back(cotangent.reshape(-1, 2 * width).astype(jnp.float32))[0].astype(
        jnp.bfloat16
    )
    part_reduce = jnp.einsum("ti,to->io", joined, grad_reduced, preferred_element_type=jnp.float32)
    grad_joined = jnp.einsum(
        "to,io->ti", grad_reduced, gathered_reduce, preferred_element_type=jnp.float32
    ).astype(jnp.bfloat16)
    grad_tokens = split_tokens(grad_joined.reshape(tile_rows // 2, tile_cols // 2, 4 * width))
    grad_rolled = roll_ahead(grad_tokens, half_win)
    grad_flat = grad_rolled.reshape(-1, width)
    grad_projected = norm_back(grad_flat.astype(jnp.float32))[0].astype(jnp.bfloat16)
    part_out = jnp.einsum("ti,to->io", attended, grad_projected, preferred_element_type=jnp.float32)
    grad_attended = jnp.einsum(
        "to,io->ti", grad_projected, gathered_out, preferred_element_type=jnp.float32
    ).astype(jnp.bfloat16)
    grad_windows = attn_back(to_windows(grad_attended.reshape(tile_rows, tile_cols, width)))[0]
    grad_qkv_rows = from_windows(grad_windows, tile_rows, tile_cols).reshape(-1, 3 * width)
    part_qkv = jnp.einsum("ti,to->io", flat_rows, grad_qkv_rows, preferred_element_type=jnp.float32)
    grad_back = jnp.einsum(
        "to,io->ti", grad_qkv_rows, gathered_qkv, preferred_element_type=jnp.float32
    )
    grad_in_rolled = (
        (grad_flat.astype(jnp.float32) + grad_back)
        .astype(jnp.bfloat16)
        .reshape(tile_rows, tile_cols, width)
    )
    grad_input = roll_behind(grad_in_rolled, half_win)
    factor = 1.0 / math.sqrt(total_rows * total_cols)
    partials = (part_qkv * factor, part_out * factor, part_reduce * factor)
    part_sums = (
        lax.psum_scatter(
            partials[0].astype(jnp.bfloat16), "narrow", scatter_dimension=1, tiled=True
        ).astype(jnp.float32),
        lax.psum_scatter(
            partials[1].astype(jnp.bfloat16), "narrow", scatter_dimension=1, tiled=True
        ).astype(jnp.float32),
        lax.psum_scatter(
            partials[2].astype(jnp.bfloat16), "narrow", scatter_dimension=1, tiled=True
        ).astype(jnp.float32),
    )
    summed_grads = (
        lax.psum_scatter(
            part_sums[0].astype(jnp.bfloat16), "wide", scatter_dimension=0, tiled=True
        ).astype(jnp.float32),
        lax.psum_scatter(
            part_sums[1].astype(jnp.bfloat16), "wide", scatter_dimension=0, tiled=True
        ).astype(jnp.float32),
        lax.psum_scatter(
            part_sums[2].astype(jnp.bfloat16), "wide", scatter_dimension=0, tiled=True
        ).astype(jnp.float32),
    )
    return (merge_local, grad_input, summed_grads[0], summed_grads[1], summed_grads[2])


def solution(mesh):
    return jax.shard_map(
        on_device,
        mesh=mesh,
        in_specs=(
            P("wide", "narrow", None),
            P("wide", "narrow"),
            P("wide", None),
            P("wide", None),
            P("wide", None),
            P(),
            P(),
            P(),
            P(),
            P(),
            P("wide", "narrow", None),
        ),
        out_specs=(
            P("wide", "narrow", None),
            P("wide", "narrow", None),
            P("wide", "narrow"),
            P("wide", "narrow"),
            P("wide", "narrow"),
        ),
        check_vma=False,
    )
```

profile of v0, /device:TPU:2, one launch (start us, length us, event | category | flops | bytes accessed | tf_op | source)
XLA Modules:
  0.0 629.7 jit_solution(15862579105998509277)
XLA Ops:
  10.7 5.8 collective-permute-start
  16.7 3.4 fusion
  21.2 42.2 %all_gather.10 = bf16[512,512]{1,0:T(8,128)(2,1)} all-gather(bf16[16,512]{1,0:T(8,128)(2,1)S(1)} %copy-done.34), channel_id=1, replica_groups=mesh['wide'=32,'narrow'=8] {'wide'}, dimensions={0}, use_global_device_ids=true | all-gather | bytes 540672 | tf_op jit(solution)/shard_map/all_gather | solution.py:148
  63.5 4.6 collective-permute-start.1
  72.7 3.5 reshape.235
  83.1 3.7 fusion.51
  99.7 8.2 %collective-permute-done.2 = bf16[4,32,512]{2,1,0:T(8,128)(2,1)S(1)} collective-permute-done((bf16[4,32,512]{2,1,0:T(8,128)(2,1)S(1)}, bf16[4,32,512]{2,1,0:T(8,128)(2,1)S(1)}, u32[]{:S(2)}, u32[]{:S(2)}) %collective-permute-start.2) | collective-permute-done | bytes 131104 | tf_op jit(solution)/shard_map/ppermute | solution.py:14
  108.2 7.2 %collective-permute-done.3 = bf16[8,4,512]{2,1,0:T(4,128)(2,1)S(1)} collective-permute-done((bf16[8,4,512]{2,1,0:T(4,128)(2,1)S(1)}, bf16[8,4,512]{2,1,0:T(4,128)(2,1)S(1)}, u32[]{:S(2)}, u32[]{:S(2)}) %collective-permute-start.3) | collective-permute-done | bytes 32800 | tf_op jit(solution)/shard_map/ppermute | solution.py:14
  121.7 6.0 all-gather.5.cloned.1.call-done
  139.6 4.0 collective-permute-start.4
  162.6 3.5 convolution_bitcast_fusion.2
  169.2 4.4 convolution_bitcast_fusion
  173.7 3.8 multiply_reduce_fusion.1
  180.4 3.7 copy.81
  184.1 3.8 convert_element_type.173
  194.4 6.5 %copy.93 = bf16[2048,1024]{0,1:T(8,128)(2,1)} copy(bf16[2048,1024]{1,0:T(8,128)(2,1)} %multiply_convert_fusion) | data formatting | bytes 8388608
  201.0 10.3 %reduce-scatter.15.cloned.1.call-done = bf16[512,64]{0,1:T(8,128)(2,1)} async-done(((bf16[512,512]{0,1:T(8,128)(2,1)}), bf16[512,64]{0,1:T(8,128)(2,1)}) %reduce-scatter.15.cloned.1.call-update) | async-done | bytes 65552 | tf_op jit(solution)/shard_map/reduce_scatter | solution.py:228
  212.9 45.9 %reduce-scatter.13.cloned.1.call-done = bf16[512,192]{0,1:T(8,128)(2,1)} async-done(((bf16[512,1536]{0,1:T(8,128)(2,1)}), bf16[512,192]{0,1:T(8,128)(2,1)}) %reduce-scatter.13.cloned.1.call-update) | async-done | bytes 196624 | tf_op jit(solution)/shard_map/reduce_scatter | solution.py:225
  260.9 92.8 %reduce-scatter.23.cloned.1.call-done = bf16[128,2048]{1,0:T(8,128)(2,1)} async-done(((bf16[1024,2048]{1,0:T(8,128)(2,1)}), bf16[128,2048]{1,0:T(8,128)(2,1)}) %reduce-scatter.23.cloned.1.call-update) | async-done | bytes 524304
  356.5 7.7 %collective-permute-done.6 = bf16[4,32,512]{2,1,0:T(8,128)(2,1)S(1)} collective-permute-done((bf16[4,32,512]{2,1,0:T(8,128)(2,1)S(1)}, bf16[4,32,512]{2,1,0:T(8,128)(2,1)S(1)}, u32[]{:S(2)}, u32[]{:S(2)}) %collective-permute-start.6) | collective-permute-done | bytes 131104 | tf_op jit(solution)/shard_map/ppermute | solution.py:14
  365.8 4.5 collective-permute-done.7
  371.1 70.2 %reduce-scatter.21.cloned.1.call-done = bf16[16,64]{1,0:T(8,128)(2,1)} async-done(((bf16[512,64]{1,0:T(8,128)(2,1)}), bf16[16,64]{1,0:T(8,128)(2,1)}) %reduce-scatter.21.cloned.1.call-update) | async-done | bytes 2064
  442.7 88.5 %reduce-scatter.19.cloned.1.call-done = bf16[16,192]{1,0:T(8,128)(2,1)} async-done(((bf16[512,192]{1,0:T(8,128)(2,1)}), bf16[16,192]{1,0:T(8,128)(2,1)}) %reduce-scatter.19.cloned.1.call-update) | async-done | bytes 6160
  532.7 88.6 %reduce-scatter.17.cloned.1.call-done = bf16[64,128]{1,0:T(8,128)(2,1)} async-done(((bf16[2048,128]{1,0:T(8,128)(2,1)}), bf16[64,128]{1,0:T(8,128)(2,1)}) %reduce-scatter.17.cloned.1.call-update) | async-done | bytes 16400 | tf_op jit(solution)/shard_map/reduce_scatter | solution.py:242
  (192 shorter events, 91.8 us)
Async XLA Ops:
  7.2 14.0 %copy-start.34 = (bf16[16,512]{1,0:T(8,128)(2,1)S(1)}, bf16[16,512]{1,0:T(8,128)(2,1)}, u32[]{:S(2)}) copy-start(bf16[16,512]{1,0:T(8,128)(2,1)} %param.14) | copy-start | bytes 49156
  7.2 62.5 %all-gather.3.cloned.1.call-start = ((), (), s32[]{:S(2)}) async-start(), calls=%async_computation.6 | async-start | bytes 1622016 | tf_op jit(solution)/shard_map/all_gather | solution.py:147
  7.9 119.8 %all-gather.5.cloned.1.call-start = ((), (), s32[]{:S(2)}) async-start(), calls=%async_computation.7 | async-start | bytes 4325376 | tf_op jit(solution)/shard_map/all_gather | solution.py:149
  8.7 202.6 %reduce-scatter.15.cloned.1.call-start = ((), (), s32[]{:S(2)}) async-start(), calls=%async_computation.9 | async-start | bytes 589824 | tf_op jit(solution)/shard_map/reduce_scatter | solution.py:228
  10.7 52.7 %collective-permute-start = (bf16[4,32,512]{2,1,0:T(8,128)(2,1)S(1)}, bf16[4,32,512]{2,1,0:T(8,128)(2,1)S(1)}, u32[]{:S(2)}, u32[]{:S(2)}) collective-permute-start(bf16[4,32,512]{2,1,0:T(8,128)(2,1)S(1)} %get-tuple-element.45), channel_id=1, source_target_pairs={{8,0},{16,8},{24,16},{32,24},{40,32},{48,40},{56,48},{64,56},{72,6... | collective-permute-start | bytes 393224 | tf_op jit(solution)/shard_map/ppermute | solution.py:14
  63.5 6.2 collective-permute-start.1
  99.4 20.5 %copy-start.35 = (f32[256]{0:T(256)}, f32[256]{0:T(256)S(1)}, u32[]{:S(2)}) copy-start(f32[256]{0:T(256)S(1)} %fusion.37) | copy-start | bytes 3076
  99.6 8.3 %collective-permute-start.2 = (bf16[4,32,512]{2,1,0:T(8,128)(2,1)S(1)}, bf16[4,32,512]{2,1,0:T(8,128)(2,1)S(1)}, u32[]{:S(2)}, u32[]{:S(2)}) collective-permute-start(bf16[4,32,512]{2,1,0:T(8,128)(2,1)S(1)} %bitcast.144), channel_id=1, source_target_pairs={{248,0},{0,8},{8,16},{16,24},{24,32},{32,40},{40,48},{48,56},{56,6... | collective-permute-start | bytes 393224 | tf_op jit(solution)/shard_map/ppermute | solution.py:14
  107.9 7.5 %collective-permute-start.3 = (bf16[8,4,512]{2,1,0:T(4,128)(2,1)S(1)}, bf16[8,4,512]{2,1,0:T(4,128)(2,1)S(1)}, u32[]{:S(2)}, u32[]{:S(2)}) collective-permute-start(bf16[8,4,512]{2,1,0:T(4,128)(2,1)S(1)} %pad_maximum_fusion.5), channel_id=1, source_target_pairs={{7,0},{0,1},{1,2},{2,3},{3,4},{4,5},{5,6},{6,7},{15,8},{8,9},{9,10... | collective-permute-start | bytes 98312 | tf_op jit(solution)/shard_map/ppermute | solution.py:14
  121.7 9.4 %copy-start.19 = (bf16[4,16,1024]{2,1,0:T(8,128)(2,1)S(1)}, bf16[4,16,1024]{2,1,0:T(8,128)(2,1)}, u32[]{:S(2)}) copy-start(bf16[4,16,1024]{2,1,0:T(8,128)(2,1)} %param.21) | copy-start | bytes 393220
  121.7 9.4 %copy-start.33 = (f32[1024]{0:T(1024)S(1)}, f32[1024]{0:T(1024)}, u32[]{:S(2)}) copy-start(f32[1024]{0:T(1024)} %param.20) | copy-start | bytes 12292
  137.0 16.0 %copy-start.36 = (f32[256]{0:T(256)S(1)}, f32[256]{0:T(256)}, u32[]{:S(2)}) copy-start(f32[256]{0:T(256)} %copy-done.35) | copy-start | bytes 3076
  139.6 7.0 %collective-permute-start.4 = (bf16[4,32,512]{2,1,0:T(8,128)(2,1)}, bf16[4,32,512]{2,1,0:T(8,128)(2,1)}, u32[]{:S(2)}, u32[]{:S(2)}) collective-permute-start(bf16[4,32,512]{2,1,0:T(8,128)(2,1)} %slice.91), channel_id=1, source_target_pairs={{8,0},{16,8},{24,16},{32,24},{40,32},{48,40},{56,48},{64,56},{72,6... | collective-permute-start | bytes 393224 | tf_op jit(solution)/shard_map/ppermute | solution.py:14
  147.6 4.0 collective-permute-start.5
  154.3 8.2 %copy-start.31 = (f32[4,16,64]{2,1,0:T(8,128)S(1)}, f32[4,16,64]{2,1,0:T(8,128)}, u32[]{:S(2)}) copy-start(f32[4,16,64]{2,1,0:T(8,128)} %copy-done.30) | copy-start | bytes 49156
  168.9 89.9 %reduce-scatter.13.cloned.1.call-start = ((), (), s32[]{:S(2)}) async-start(), calls=%async_computation.8 | async-start | bytes 1769472 | tf_op jit(solution)/shard_map/reduce_scatter | solution.py:225
  191.0 162.8 %reduce-scatter.23.cloned.1.call-start = ((), (), s32[]{:S(2)}) async-start(), calls=%async_computation.13 | async-start | bytes 4718592
  200.9 154.9 %copy-start.8 = (bf16[8,32,512]{2,1,0:T(8,128)(2,1)S(1)}, bf16[8,32,512]{2,1,0:T(8,128)(2,1)}, u32[]{:S(2)}) copy-start(bf16[8,32,512]{2,1,0:T(8,128)(2,1)} %copy-done.7) | copy-start | bytes 786436
  200.9 154.9 %copy-start.15 = (bf16[512,1536]{1,0:T(8,128)(2,1)S(1)}, bf16[512,1536]{1,0:T(8,128)(2,1)}, u32[]{:S(2)}) copy-start(bf16[512,1536]{1,0:T(8,128)(2,1)} %all-gather.3.cloned.1.call-done) | copy-start | bytes 4718596
  200.9 240.4 %reduce-scatter.21.cloned.1.call-start = ((), (), s32[]{:S(2)}) async-start(), calls=%async_computation.12 | async-start | bytes 135168
  212.9 318.3 %reduce-scatter.19.cloned.1.call-start = ((), (), s32[]{:S(2)}) async-start(), calls=%async_computation.11 | async-start | bytes 270336
  260.6 360.6 %reduce-scatter.17.cloned.1.call-start = ((), (), s32[]{:S(2)}) async-start(), calls=%async_computation.10 | async-start | bytes 540672 | tf_op jit(solution)/shard_map/reduce_scatter | solution.py:242
  356.5 7.7 %collective-permute-start.6 = (bf16[4,32,512]{2,1,0:T(8,128)(2,1)S(1)}, bf16[4,32,512]{2,1,0:T(8,128)(2,1)S(1)}, u32[]{:S(2)}, u32[]{:S(2)}) collective-permute-start(bf16[4,32,512]{2,1,0:T(8,128)(2,1)S(1)} %bitcast.145), channel_id=1, source_target_pairs={{248,0},{0,8},{8,16},{16,24},{24,32},{32,40},{40,48},{48,56},{56,6... | collective-permute-start | bytes 393224 | tf_op jit(solution)/shard_map/ppermute | solution.py:14
  364.2 6.1 collective-permute-start.7
  (33 other events, 108.1 us)
Sparse Core Ops, SparseCore 0:
  10.6 55.8 all-gather.2
  69.0 58.7 all-gather.4
  169.0 42.2 reduce-scatter.14
  213.9 44.8 reduce-scatter.12
  261.4 92.3 reduce-scatter.22
  357.8 83.4 reduce-scatter.20
  445.5 85.6 reduce-scatter.18
  535.4 85.8 reduce-scatter.16
where the time goes:
time: 636 us; the launch traced here: 630 us
  waiting for transfers between devices  435 us (68%)
  local copies, waits for them, and re-layouts  63.3 us (10%)
  blocking collectives  42.2 us (7%)
  matrix products  40.8 us (6%)
  starting transfers between devices  18.8 us (3%)
  between operations  15.1 us (2%)
  other arithmetic  14.8 us (2%)
    unnamed x11, waiting for transfers between devices  253 us
    reduce_scatter x1, waiting for transfers between devices, on_device(): lax.psum_scatter(part_sums[2].astype(jnp.bfloat16), 'wide', scatter_dimen...  88.6 us
    reduce_scatter x1, waiting for transfers between devices, on_device(): lax.psum_scatter(partials[0].astype(jnp.bfloat16), 'narrow', scatter_dime...  45.9 us
    all_gather x1, blocking collectives, on_device(): lax.all_gather(w_out, 'wide', axis=0, tiled=True)  42.2 us
    ppermute x8, waiting for transfers between devices, from_behind(): return lax.ppermute(block, axis, route)  31 us
    unnamed x91, local copies, waits for them, and re-layouts  19.3 us
    ppermute x8, starting transfers between devices, from_behind(): return lax.ppermute(block, axis, route)  18 us
  transfers between devices with their start and end apart: 16, of which 14 were waited for; matrix products, arithmetic and copies ran while one was open for 14% of the time, Pallas kernels for 0%

commit v1 on v0

v1 whole, which is shorter than its diff:
```python
import jax
import jax.numpy as jnp
import numpy as np
from jax import lax
from jax.experimental import pallas as pl
from jax.experimental.pallas import tpu as pltpu
from jax.sharding import PartitionSpec as P

MESH = pl.DeviceIdType.MESH
F32 = jnp.float32
BF16 = jnp.bfloat16
NT = (((1,), (1,)), ((), ()))
TN = (((0,), (0,)), ((), ()))


def one_hot(sources):
    sources = np.asarray(sources).reshape(-1)
    table = np.zeros((len(sources), len(sources)), np.float32)
    table[np.arange(len(sources)), sources] = 1.0
    return table


def token_tables():
    i, j, r, c = np.meshgrid(*map(np.arange, (2, 8, 4, 4)), indexing="ij")
    block_from_natural = one_hot((4 * i + r) * 32 + 4 * j + c)
    k, win, mr, mc = np.meshgrid(*map(np.arange, (4, 4, 4, 4)), indexing="ij")
    i, r = mr // 2, 2 * (mr % 2) + k % 2
    j, c = 2 * win + mc // 2, 2 * (mc % 2) + k // 2
    merge_from_block = one_hot((i * 8 + j) * 16 + r * 4 + c)
    i, j, q, m = np.meshgrid(*map(np.arange, (2, 8, 4, 4)), indexing="ij")
    cot_block_from_natural = one_hot(q * 64 + (2 * i + m // 2) * 16 + 2 * j + m % 2)
    q, win, mr, mc = np.meshgrid(*map(np.arange, (4, 4, 4, 4)), indexing="ij")
    i, j, m = mr // 2, 2 * win + mc // 2, (mr % 2) * 2 + mc % 2
    cot_merge_from_block = one_hot((i * 8 + j) * 16 + q * 4 + m)
    return (
        block_from_natural,
        merge_from_block,
        cot_block_from_natural,
        cot_merge_from_block,
    )


def window_tables():
    k, mr, mc = np.meshgrid(*map(np.arange, (4, 4, 4)), indexing="ij")
    row, col = (2 * mr + k % 2).reshape(-1), (2 * mc + k // 2).reshape(-1)
    order = one_hot(row * 8 + col)
    row_cut = (row[:, None] >= 4) != (row[None, :] >= 4)
    col_cut = (col[:, None] >= 4) != (col[None, :] >= 4)
    tiled = lambda cut: np.tile(cut.astype(np.float32), (1, 4))
    return order, tiled(row_cut), tiled(col_cut)


def same_block(rows, row_size, cols, col_size):
    return (
        (np.arange(rows) // row_size)[:, None] == (np.arange(cols) // col_size)[None]
    ).astype(np.float32)


T_BLOCK, T_MERGE, T_CBLOCK, T_CMERGE = token_tables()
COLUMNS_64 = one_hot(np.arange(512).reshape(4, 2, 64).transpose(1, 0, 2)).T
COLUMNS_16 = one_hot(np.arange(512).reshape(16, 2, 16).transpose(1, 0, 2)).T
WIN_ORDER, ROW_CUT, COL_CUT = window_tables()


def const(table, dtype=BF16):
    return jnp.asarray(table, dtype)


class Place:
    def __init__(self):
        wide, narrow = lax.axis_index("wide"), lax.axis_index("narrow")
        self.wide, self.narrow = wide, narrow
        self.core = lax.rem(wide, 2)
        self.zh = lax.rem(lax.div(wide, 2), 4)
        self.x = lax.div(wide, 8)
        self.y = lax.div(narrow, 2)
        self.zl = lax.rem(narrow, 2)
        self.z = 2 * self.zh + self.zl
        self.sibling = (wide + 1 - 2 * self.core, narrow)

    def at_x(self, step):
        return ((lax.rem(self.x + step + 4, 4) * 4 + self.zh) * 2 + self.core, self.narrow)

    def at_y(self, step):
        return (self.wide, lax.rem(self.y + step + 4, 4) * 2 + self.zl)

    def at_z(self, step):
        z = lax.rem(self.z + step + 8, 8)
        return ((self.x * 4 + lax.div(z, 2)) * 2 + self.core, self.y * 2 + lax.rem(z, 2))

    def at_tile(self, rows, cols):
        return (lax.rem(self.wide + rows + 32, 32), lax.rem(self.narrow + cols + 8, 8))


class Sender:
    def __init__(self, send_sem, recv_sem, local_sem):
        self.send_sem, self.recv_sem, self.local_sem = send_sem, recv_sem, local_sem
        self.started, self.count, self.local_count = [], 0, 0

    def remote(self, src, dst, device):
        copy = pltpu.make_async_remote_copy(
            src_ref=src,
            dst_ref=dst,
            send_sem=self.send_sem.at[self.count],
            recv_sem=self.recv_sem.at[self.count],
            device_id=device,
            device_id_type=MESH,
        )
        self.count += 1
        copy.start()
        self.started.append(copy)
        return copy

    def local(self, src, dst):
        copy = pltpu.make_async_copy(src, dst, self.local_sem.at[self.local_count])
        self.local_count += 1
        copy.start()
        return copy

    def drain(self):
        for copy in self.started:
            copy.wait_send()
        self.started = []


def greet(devices):
    barrier = pltpu.get_barrier_semaphore()
    for device in devices:
        pl.semaphore_signal(barrier, inc=1, device_id=device, device_id_type=MESH)
    pl.semaphore_wait(barrier, len(devices))


def lanes(start, size):
    return pl.ds(pl.multiple_of(start, 128), size)


def mm(a, b):
    return jnp.dot(a, b, preferred_element_type=F32)


def dg(a, b, dims):
    return lax.dot_general(a, b, dims, preferred_element_type=F32)


def add(*parts):
    total = parts[0].astype(F32)
    for one in parts[1:]:
        total = total + one.astype(F32)
    return total


def split_mm(values, table):
    high = values.astype(BF16)
    low = (values - high.astype(F32)).astype(BF16)
    both = mm(jnp.concatenate([high, low], 0), table)
    return both[: len(values)] + both[len(values) :]


def norm_parts(values):
    centred = values - jnp.mean(values, -1, keepdims=True)
    scale = lax.rsqrt(jnp.mean(centred * centred, -1, keepdims=True) + 1e-05)
    return centred * scale, scale


def norm_back(cot, normed, scale, gain):
    cot = cot * gain
    shared = jnp.mean(cot, -1, keepdims=True) + normed * jnp.mean(cot * normed, -1, keepdims=True)
    return scale * (cot - shared)


EVERY = pl.ds(0, 4)


class Gather:
    def __init__(self, at, go, shard, whole, cut, quarters=False, direct=False):
        self.at, self.go, self.shard, self.whole, self.cut = at, go, shard, whole, cut
        self.quarters, self.direct = quarters, direct
        self.x_left, self.x_right, self.x_far = (lax.rem(at.x + step, 4) for step in (3, 1, 2))
        self.y_left, self.y_right, self.y_far = (lax.rem(at.y + step, 4) for step in (3, 1, 2))
        self.shared = []

    def part(self, xs, zs, y=None):
        y = self.at.y if y is None else y
        return self.whole.at[(xs, zs, self.at.core) + self.cut(y)]

    def move(self, xs, zs, device, y=None):
        ref = self.part(xs, zs, y)
        return self.go.remote(ref, ref, device)

    def share(self, xs, zs, y=None):
        self.shared.append(self.move(xs, zs, self.at.sibling, y))

    def start(self):
        at = self.at
        own, there = self.shard.at[self.cut(at.y)], self.part(at.x, at.zh)
        way = 2 * at.zl - 1
        self.z = [self.go.remote(own, there, at.at_z(way * step)) for step in (1, 2, 3)]
        self.mine = self.go.local(own, there)

    def x1(self):
        at = self.at
        self.mine.wait()
        for copy in self.z:
            copy.wait_recv()
        steps = (1, 2, -1) if self.direct else (1, -1)
        self.x = [self.move(at.x, EVERY, at.at_x(step)) for step in steps]
        if not self.quarters:
            self.share(at.x, EVERY)

    def x2(self):
        at = self.at
        self.x[0].wait_recv()
        far = [self.move(self.x_left, pl.ds(0, 2), at.at_x(1))]
        self.x[1].wait_recv()
        far.append(self.move(self.x_right, pl.ds(2, 2), at.at_x(-1)))
        self.x = far
        if not self.quarters:
            self.share(self.x_left, EVERY)
            self.share(self.x_right, EVERY)

    def x3(self):
        for copy in self.x:
            copy.wait_recv()
        if not self.quarters:
            self.share(self.x_far, EVERY)

    def y1(self):
        at = self.at
        self.x3()
        self.y = [self.move(EVERY, EVERY, at.at_y(step)) for step in (1, -1)]
        self.share(EVERY, EVERY)

    def y2(self):
        at = self.at
        self.y[0].wait_recv()
        far = [self.move(pl.ds(0, 2), EVERY, at.at_y(1), self.y_left)]
        self.y[1].wait_recv()
        far.append(self.move(pl.ds(2, 2), EVERY, at.at_y(-1), self.y_right))
        self.y = far
        self.share(EVERY, EVERY, self.y_left)
        self.share(EVERY, EVERY, self.y_right)

    def y3(self):
        for copy in self.y:
            copy.wait_recv()
        self.share(EVERY, EVERY, self.y_far)

    def done(self):
        for copy in self.shared:
            copy.wait_recv()


def y_cut(j):
    return lanes(j * 256, 256)


class Reduce:
    def __init__(self, at, go, m, bx1, bx2, by1, by2, cx, cy, dx, dy, zsend, zland):
        self.at, self.go, self.m = at, go, m
        self.bx1, self.bx2, self.by1, self.by2 = bx1, bx2, by1, by2
        self.cx, self.cy = cx, cy
        self.dx, self.dy = dx, dy
        self.zsend, self.zland = zsend, zland
        self.xs = [lax.rem(at.x + step, 4) for step in (2, 1, 3, 0)]
        self.ys = [lax.rem(at.y + step, 4) for step in (2, 1, 3, 0)]
        self.x_left, self.x_right = at.at_x(-1), at.at_x(1)
        self.y_left, self.y_right = at.at_y(-1), at.at_y(1)

    def both(self, src, dst, right, left, step):
        if step == 1:
            pairs = ((src(0, pl.ds(0, 2)), right), (src(0, pl.ds(2, 2)), left))
        else:
            pairs = ((src(1, EVERY), right), (src(2, EVERY), left))
        return [self.go.remote(ref, dst.at[n], device) for n, (ref, device) in enumerate(pairs)]

    def x_src(self, n, part):
        return self.m.at[0, self.xs[n], part]

    def y_src(self, n, part):
        return self.m.at[1, part, :, :, y_cut(self.ys[n])]

    def first_x(self):
        self.b_x = self.both(self.x_src, self.bx1, self.x_right, self.x_left, 1)

    def first_y(self):
        self.b_y = self.both(self.y_src, self.by1, self.y_right, self.y_left, 1)

    def second_x(self):
        m, xs = self.m, self.xs
        for copy in self.b_x:
            copy.wait_recv()
        for s in range(2):
            m[0, xs[1], s] = add(m[0, xs[1], s], self.bx1[0, s]).astype(BF16)
            m[0, xs[2], 2 + s] = add(m[0, xs[2], 2 + s], self.bx1[1, s]).astype(BF16)
        self.b_x = self.both(self.x_src, self.bx2, self.x_right, self.x_left, 2)

    def second_y(self):
        m, ys = self.m, self.ys
        for copy in self.b_y:
            copy.wait_recv()
        for s in range(2):
            cut = y_cut(ys[1])
            m[1, s, :, :, cut] = add(m[1, s, :, :, cut], self.by1[0, s]).astype(BF16)
            cut = y_cut(ys[2])
            m[1, 2 + s, :, :, cut] = add(m[1, 2 + s, :, :, cut], self.by1[1, s]).astype(BF16)
        self.b_y = self.both(self.y_src, self.by2, self.y_right, self.y_left, 2)

    def third_x(self):
        at = self.at
        for copy in self.b_x:
            copy.wait_recv()
        for s in range(4):
            self.cx[s] = add(self.m[0, at.x, s], self.bx2[0, s], self.bx2[1, s]).astype(BF16)
        self.d = []
        for n, step in ((0, 2), (1, 1), (2, 3)):
            src = self.cx.at[:, :, y_cut(self.ys[n])]
            self.d.append(self.go.remote(src, self.dx.at[n], at.at_y(step)))

    def third_y(self):
        at = self.at
        for copy in self.b_y:
            copy.wait_recv()
        for s in range(4):
            self.cy[s] = add(self.m[1, s, :, :, y_cut(at.y)], self.by2[0, s], self.by2[1, s]).astype(BF16)
        for n, step in ((0, 2), (1, 1), (2, 3)):
            self.d.append(self.go.remote(self.cy.at[self.xs[n]], self.dy.at[n], at.at_x(step)))

    def fourth(self, pack):
        for copy in self.d:
            copy.wait_recv()
        for h in range(4):
            a = add(self.cx[h, :, y_cut(self.at.y)], *[self.dx[n, h] for n in range(3)])
            b = add(self.cy[self.at.x, h], *[self.dy[n, h] for n in range(3)])
            for low in range(2):
                self.zsend[h, low] = pack(a, b, low).astype(BF16)
        self.last = []
        for step in range(1, 8):
            z = lax.rem(self.at.z + step, 8)
            src = self.zsend.at[lax.div(z, 2), lax.rem(z, 2)]
            self.last.append(self.go.remote(src, self.zland.at[step - 1], self.at.at_z(step)))

    def fifth(self):
        total = self.zsend[self.at.zh, self.at.zl].astype(F32)
        for step in range(7):
            self.last[step].wait_recv()
            total = total + self.zland[step].astype(F32)
        return total


def pack_reduce(a, b, low):
    cut = slice(128 * low, 128 * low + 128)
    return jnp.concatenate([a[:, cut], b[:, cut]], 0)


def pack_qkv_out(a, b, low):
    if low == 0:
        rows = a[:, 0:128], jnp.concatenate([a[:, 128:192], b[:, 128:192]], 1)
    else:
        rows = (
            jnp.concatenate([a[:, 192:256], b[:, 0:64]], 1),
            jnp.concatenate([b[:, 64:128], b[:, 192:256]], 1),
        )
    return jnp.concatenate(rows, 0)


def reduce_scratch(rows, z_rows):
    return [
        pltpu.VMEM((2, 2, rows, 1024), BF16),
        pltpu.VMEM((2, 4, rows, 1024), BF16),
        pltpu.VMEM((2, 2, 4, rows, 256), BF16),
        pltpu.VMEM((2, 4, 4, rows, 256), BF16),
        pltpu.VMEM((4, rows, 1024), BF16),
        pltpu.VMEM((4, 4, rows, 256), BF16),
        pltpu.VMEM((3, 4, rows, 256), BF16),
        pltpu.VMEM((3, 4, rows, 256), BF16),
        pltpu.VMEM((4, 2, z_rows, 128), BF16),
        pltpu.VMEM((7, z_rows, 128), BF16),
    ]


COPIES = 12 + 18 + 3 * 11 + 15 + 8 + 2 * (8 + 6 + 7) + 16


def block_kernel(
    stash_ref, exp_ref, cot_ref, wq_ref, wo_ref, wr_ref, ls_ref, table_ref, rel_ref, ng_ref, mg_ref,
    t_block_ref, t_cblock_ref, order_ref, row_cut_ref, col_cut_ref, *rest,
):
    tables, rest = rest[:11], rest[11:]
    (
    merged_ref, gin_ref, gq_ref, go_ref, gr_ref,
    blk, land, back, oland, ocland, wq, wo, wr,
    x_tok, cot_tok, qkv, qs, kh, rq, rk, probs, bias, bias_rows, table, mask, att, d_att, dqs, dkh, dqkv,
    xhat, xscale, ro, dproj, dtok, xt, at_t, ls_row, ro_cols, ro_theirs, x_cols, x_theirs, at_cols, at_theirs,
    dred, dred_theirs, dproj_theirs, dqkv_theirs, fa, fb, mb,
    t_merge_ref, t_cmerge_ref, t_unblock_ref, t_unmerge_ref, t_cunblock_ref, t_cunmerge_ref,
    columns_ref, columns_16_ref, bd64_ref, bd32_ref, heads_ref,
    *rest,
    ) = rest
    a_bufs, b_bufs, (send_sem, recv_sem, local_sem) = rest[0:10], rest[10:20], rest[20:]
    held = (
        t_merge_ref, t_cmerge_ref, t_unblock_ref, t_unmerge_ref, t_cunblock_ref, t_cunmerge_ref,
        columns_ref, columns_16_ref, bd64_ref, bd32_ref, heads_ref,
    )
    go = Sender(send_sem, recv_sem, local_sem)
    table_copies = [go.local(src, dst) for src, dst in zip(tables, held)]
    at = Place()
    c = at.core
    greet(
        [at.sibling]
        + [at.at_x(step) for step in (1, 2, 3)]
        + [at.at_y(step) for step in (1, 2, 3)]
        + [at.at_z(step) for step in range(1, 8)]
        + [at.at_tile(*step) for step in ((-1, 0), (0, -1), (-1, -1), (1, 0), (0, 1), (1, 1))]
    )
    all_rows = pl.ds(0, 16)
    q_y = Gather(at, go, wq_ref, wq, lambda y: (all_rows, lanes(512 + 256 * y, 256)), True, True)
    q_x = Gather(at, go, wq_ref, wq, lambda y: (all_rows, pl.ds(0, 512)))
    o_x = Gather(at, go, wo_ref, wo, lambda y: (all_rows, pl.ds(0, 512)))
    r_x = Gather(at, go, wr_ref, wr, lambda y: (pl.ds(0, 64), pl.ds(0, 512)))
    r_y = Gather(at, go, wr_ref, wr, lambda y: (pl.ds(pl.multiple_of(16 * y, 16), 16), pl.ds(512, 512)), True)

    q_y.start()

    factor_of = exp_ref[...]
    factor_of = jnp.where(factor_of == -8, 2.0**-8, jnp.where(factor_of == -7, 2.0**-7, 2.0**-6))
    in_window = lax.broadcasted_iota(jnp.int32, (32, 512), 0) // 8
    factor = jnp.zeros((32, 512), F32)
    for w in range(4):
        factor = jnp.where(in_window == w, factor_of[:, w : w + 1], factor)
    inputs = stash_ref[...].astype(F32) * factor[None]
    blk[:, 0:512] = mm(t_block_ref[...], inputs.reshape(256, 512).astype(BF16)).astype(BF16)
    r_y.start()
    cot = cot_ref[...].astype(F32).reshape(64, 1024).astype(BF16)
    cot = jnp.concatenate([cot[:, 256 * q : 256 * q + 256] for q in range(4)], 0)
    blk[:, 512:768] = mm(t_cblock_ref[...], cot).astype(BF16)
    q_x.start()
    q_y.x1()
    r_x.start()
    r_y.x1()
    q_x.x1()
    o_x.start()
    q_y.y1()
    q_x.x2()

    table[...] = jnp.zeros((16, 256), F32)
    table[:, 0:225] = 16.0 * jax.nn.sigmoid(table_ref[...])
    by_head = table[...]
    high = by_head.astype(BF16)
    low = (by_head - high.astype(F32)).astype(BF16)
    both = jnp.concatenate([high, low], 0)
    rel = mm(order_ref[...], rel_ref[...].astype(F32).astype(BF16)).astype(BF16)
    rel = dg(rel, order_ref[...], NT).astype(jnp.int32)
    rel = jnp.concatenate([rel[16 * j : 16 * j + 16] for j in range(4)], 1)
    entry = lax.broadcasted_iota(jnp.int32, (256, 256), 0)

    def bias_of(rows):
        for a in rows:
            chosen = jnp.where(entry == rel[a : a + 1], 1.0, 0.0).astype(BF16)
            got = mm(both, chosen)
            got = got[0:16] + got[16:32]
            for j in range(4):
                bias_rows[16 * j + a] = got[:, 64 * j : 64 * j + 64]

    bias_of(range(0, 5))
    r_y.x2()
    halo = [
        go.remote(blk.at[pl.ds(16, 112)], land.at[pl.ds(128, 112)], at.at_tile(-1, 0)),
        go.remote(blk.at[pl.ds(128, 16)], land.at[pl.ds(112, 16)], at.at_tile(0, -1)),
        go.remote(blk.at[pl.ds(0, 16)], land.at[pl.ds(240, 16)], at.at_tile(-1, -1)),
    ]
    r_x.x1()
    bias_of(range(5, 10))
    q_y.y2()
    q_x.x3()
    r_y.y1()
    bias_of(range(10, 16))
    o_x.x1()
    q_y.y3()
    for g in range(4):
        bias[g] = jnp.concatenate([bias_rows[:, 4 * g + h, :] for h in range(4)], 1)
    last_rows = (at.wide == 31).astype(F32)
    last_cols = (at.narrow == 7).astype(F32)
    mask[0] = row_cut_ref[...] * last_rows * -100.0
    mask[1] = jnp.maximum(row_cut_ref[...] * last_rows, col_cut_ref[...] * last_cols) * -100.0
    lane = lax.broadcasted_iota(jnp.int32, (1, 512), 1) // 32
    scales = jnp.zeros((1, 512), F32)
    for h in range(16):
        scales = jnp.where(lane == h, ls_ref[:, h : h + 1], scales)
    ls_row[...] = scales


    for copy in halo:
        copy.wait_recv()
    for copy in table_copies:
        copy.wait()
    r_x.x2()
    land[pl.ds(0, 112)] = blk[pl.ds(144, 112)]
    x_tok[...] = mm(t_merge_ref[...], land[:, 0:512]).astype(BF16)
    cot = mm(t_cmerge_ref[...], land[:, 512:768]).astype(BF16)
    cot_tok[...] = jnp.concatenate([cot[64 * q : 64 * q + 64] for q in range(4)], 1)
    x_cols[...] = mm(x_tok[...], columns_16_ref[...]).astype(BF16)
    not_mine = lanes(256 * (1 - c), 256)
    mine = lanes(256 * c, 256)
    x_swap = go.remote(x_cols.at[:, not_mine], x_theirs, at.sibling)
    q_x.done()
    o_x.x2()
    q_y.done()
    r_y.y2()

    qkv[...] = mm(x_tok[...], wq[...].reshape(512, 1536)).astype(BF16)
    r_x.x3()
    o_x.x3()
    for start, inverse, unit in ((0, rq, qs), (512, rk, kh)):
        for n in range(2):
            cut = slice(256 * n, 256 * n + 256)
            for row in range(0, 256, 128):
                rows = slice(row, row + 128)
                raw = qkv[rows, start + 256 * n : start + 256 * n + 256].astype(F32)
                inv = lax.rsqrt(jnp.maximum(split_mm(raw * raw, bd32_ref[...]), 1e-24))
                inverse[rows, cut] = inv
                raw = raw * inv
                if start == 0:
                    raw = raw * ls_row[:, cut]
                unit[rows, cut] = raw.astype(BF16)
    x_swap.wait_recv()
    xt[:, 0:256] = x_cols[:, mine].T
    xt[:, 256:512] = x_theirs[...].T

    def window(ref, win, cut):
        return jnp.concatenate([ref[pl.ds(64 * k + 16 * win, 16), cut] for k in range(4)], 0)

    def put_window(ref, win, cut, values):
        for k in range(4):
            ref[pl.ds(64 * k + 16 * win, 16), cut] = values[16 * k : 16 * k + 16]

    def spread(rows):
        return jnp.concatenate([rows] * 4, 0) * heads_ref[...]

    def fold(values):
        values = values * heads_ref[...].astype(F32)
        return (values[0:64] + values[64:128]) + (values[128:192] + values[192:256])

    def forward(g):
        cut = slice(g * 128, g * 128 + 128)
        v_cut = slice(g * 128 + 1024, g * 128 + 1152)
        weights = []
        for win in range(4):
            scores = dg(window(qs, win, cut), spread(window(kh, win, cut)), NT)
            weights.append(jnp.exp(scores + bias[g] + mask[1 if win == 3 else 0]))
        totals = split_mm(jnp.concatenate(weights, 0), bd64_ref[...])
        for win in range(4):
            p = weights[win] / totals[64 * win : 64 * win + 64]
            probs[g, win] = p
            values = spread(window(qkv, win, v_cut))
            put_window(att, win, cut, mm(p.astype(BF16), values).astype(BF16))

    forward(0)
    forward(1)
    r_y.y3()
    forward(2)
    forward(3)
    r_x.done()
    at_cols[...] = mm(att[...], columns_16_ref[...]).astype(BF16)
    at_swap = go.remote(at_cols.at[:, not_mine], at_theirs, at.sibling)
    o_x.done()
    xhat[...] = mm(att[...], wo[...].reshape(512, 512))
    for row in range(0, 256, 64):
        rows = slice(row, row + 64)
        normed, scale = norm_parts(xhat[rows])
        xhat[rows] = normed
        xscale[rows] = scale
        ro[rows] = (x_tok[rows].astype(F32) + normed * ng_ref[...]).astype(BF16)
    ro_cols[...] = mm(ro[...], columns_ref[...]).astype(BF16)
    swap = [go.remote(ro_cols.at[:, not_mine], ro_theirs, at.sibling)]
    r_y.done()

    reduced = jnp.zeros((64, 1024), F32)
    for k in range(4):
        reduced += mm(ro[64 * k : 64 * k + 64], wr[k].reshape(512, 1024))
    normed, scale = norm_parts(reduced)
    dred[...] = norm_back(cot_tok[...].astype(F32), normed, scale, mg_ref[...]).astype(BF16)
    swap.append(go.remote(dred, dred_theirs, at.sibling))
    merged = (normed * mg_ref[...]).astype(BF16)
    merged = jnp.concatenate([merged[:, 256 * q : 256 * q + 256] for q in range(4)], 0)
    mb[...] = mm(t_cunmerge_ref[...], merged).astype(BF16)

    def send_back(tile, landing):
        return [
            go.remote(tile.at[pl.ds(128, 112)], landing.at[pl.ds(16, 112)], at.at_tile(1, 0)),
            go.remote(tile.at[pl.ds(112, 16)], landing.at[pl.ds(128, 16)], at.at_tile(0, 1)),
            go.remote(tile.at[pl.ds(240, 16)], landing.at[pl.ds(0, 16)], at.at_tile(1, 1)),
        ]

    for k in range(4):
        dtok[64 * k : 64 * k + 64] = dg(dred[...], wr[k].reshape(512, 1024), NT).astype(BF16)

    for copy in swap:
        copy.wait_recv()
    a_sum = Reduce(at, go, fa, *a_bufs)
    grads = jnp.concatenate([dred[...], dred_theirs[...]], 0)
    for n in range(4):
        k = a_sum.xs[n]
        rows = pl.ds(pl.multiple_of(64 * k, 64), 64)
        tokens = jnp.concatenate([ro_cols[rows, mine], ro_theirs[rows]], 0).T
        for cut in (slice(0, 512), slice(512, 1024)):
            got = mm(tokens, grads[:, cut]).astype(BF16).reshape(4, 64, 512)
            fa[0, k, :, :, cut] = got[:, 0:32]
            fa[1, k, :, :, cut] = got[:, 32:64]
        if n == 0:
            a_sum.first_x()
    a_sum.first_y()
    merged_back = send_back(mb, ocland)

    for row in range(0, 256, 64):
        rows = slice(row, row + 64)
        got = norm_back(dtok[rows].astype(F32), xhat[rows], xscale[rows], ng_ref[...])
        dproj[rows] = got.astype(BF16)
    dproj_swap = go.remote(dproj, dproj_theirs, at.sibling)
    a_sum.second_x()
    at_swap.wait_recv()
    at_t[:, 0:256] = at_cols[:, mine].T
    at_t[:, 256:512] = at_theirs[...].T
    d_att[...] = dg(dproj[...], wo[...].reshape(512, 512), NT).astype(BF16)
    a_sum.second_y()

    def backward(g):
        cut = slice(g * 128, g * 128 + 128)
        v_cut = slice(g * 128 + 1024, g * 128 + 1152)
        dps = []
        for win in range(4):
            dp = dg(window(d_att, win, cut), spread(window(qkv, win, v_cut)), NT)
            dps.append(dp.astype(BF16).astype(F32))
        alike = split_mm(jnp.concatenate([probs[g, win] * dps[win] for win in range(4)], 0), bd64_ref[...])
        for win in range(4):
            p = probs[g, win]
            ds = (p * (dps[win] - alike[64 * win : 64 * win + 64])).astype(BF16)
            put_window(dqs, win, cut, mm(ds, spread(window(kh, win, cut))))
            put_window(dkh, win, cut, fold(dg(ds, window(qs, win, cut), TN)))
            put_window(dqkv, win, v_cut, fold(dg(p.astype(BF16), window(d_att, win, cut), TN)).astype(BF16))

    for g in range(4):
        backward(g)

    def swap_dqkv(start):
        cut = pl.ds(start, 512)
        return go.remote(dqkv.at[:, cut], dqkv_theirs.at[:, cut], at.sibling)

    dqkv_swap = [swap_dqkv(1024)]
    for start, inverse, grad in ((0, rq, dqs), (512, rk, dkh)):
        for n in range(2):
            cut = slice(256 * n, 256 * n + 256)
            both_cut = slice(start + 256 * n, start + 256 * n + 256)
            for row in range(0, 256, 128):
                rows = slice(row, row + 128)
                inv = inverse[rows, cut]
                unit = qkv[rows, both_cut].astype(F32) * inv
                d_unit = grad[rows, cut]
                if start == 0:
                    d_unit = d_unit * ls_row[:, cut]
                along = split_mm(unit * d_unit, bd32_ref[...])
                along = jnp.where(inv < 1e12, along, 0.0)
                dqkv[rows, both_cut] = (inv * (d_unit - unit * along)).astype(BF16)
        dqkv_swap.append(swap_dqkv(start))
    a_sum.third_x()
    dproj_swap.wait_recv()
    d_out = jnp.concatenate([dproj[...], dproj_theirs[...]], 0)
    out = mm(at_t[...], d_out).astype(BF16)
    for y in range(4):
        fb[1, :, :, :, 256 * y + 128 : 256 * y + 256] = out[:, 128 * y : 128 * y + 128].reshape(4, 4, 16, 128)

    for copy in dqkv_swap:
        copy.wait_recv()
    b_sum = Reduce(at, go, fb, *b_bufs)
    for n in range(4):
        y = b_sum.ys[n]
        cut = lanes(384 * y, 384)
        grads = jnp.concatenate([dqkv[:, cut], dqkv_theirs[:, cut]], 0)
        got = mm(xt[...], grads).astype(BF16)
        fb[0, :, :, :, y_cut(y)] = got[:, 0:256].reshape(4, 4, 16, 256)
        fb[1, :, :, :, lanes(256 * y, 128)] = got[:, 256:384].reshape(4, 4, 16, 128)
    b_sum.first_x()
    b_sum.first_y()
    a_sum.third_y()
    d_in = dtok[...].astype(F32) + dg(dqkv[...], wq[...].reshape(512, 1536), NT)
    back[...] = mm(t_unmerge_ref[...], d_in.astype(BF16)).astype(BF16)
    grad_back = send_back(back, oland)
    b_sum.second_x()
    b_sum.second_y()
    a_sum.fourth(pack_reduce)
    for copy in grad_back:
        copy.wait_recv()
    oland[pl.ds(144, 112)] = back[pl.ds(0, 112)]
    b_sum.third_x()
    b_sum.third_y()
    b_sum.fourth(pack_qkv_out)
    for copy in merged_back:
        copy.wait_recv()
    ocland[pl.ds(144, 112)] = mb[pl.ds(0, 112)]
    got = mm(t_cunblock_ref[...], ocland[...]).astype(BF16)
    for q in range(4):
        merged_ref[:, :, 256 * q : 256 * q + 256] = got[64 * q : 64 * q + 64].reshape(4, 16, 256)
    gin_ref[...] = mm(t_unblock_ref[...], oland[...]).astype(BF16).reshape(8, 32, 512)
    factor = 1.0 / 256.0
    gr_ref[...] = a_sum.fifth() * factor
    go.drain()
    total = b_sum.fifth() * factor
    gq_ref[:, 0:128] = total[0:16]
    gq_ref[:, 128:192] = total[16:32, 0:64]
    go_ref[...] = total[16:32, 64:128]


def hand_on(*refs):
    for src, dst in zip(refs[:5], refs[5:]):
        dst[...] = src[...]


def on_device(
    stash_values, scale_exp, w_qkv, w_out, w_reduce, logit_scale, bias_table, rel_index, norm_gain, merge_gain, cotangent
):
    vmem = pl.BlockSpec(memory_space=pltpu.VMEM)
    sems = pltpu.SemaphoreType.DMA
    outputs = (
        jax.ShapeDtypeStruct((4, 16, 1024), BF16),
        jax.ShapeDtypeStruct((8, 32, 512), BF16),
        jax.ShapeDtypeStruct((16, 192), F32),
        jax.ShapeDtypeStruct((16, 64), F32),
        jax.ShapeDtypeStruct((64, 128), F32),
    )
    tokens = lambda width, kind=BF16: pltpu.VMEM((256, width), kind)
    results = pl.pallas_call(
        block_kernel,
        out_shape=outputs,
        in_specs=[vmem] * 16 + [pl.BlockSpec(memory_space=pl.ANY)] * 11,
        out_specs=(vmem,) * 5,
        scratch_shapes=[
            tokens(768), tokens(768), tokens(512), tokens(512), tokens(256),
            pltpu.VMEM((4, 4, 2, 16, 1536), BF16),
            pltpu.VMEM((4, 4, 2, 16, 512), BF16),
            pltpu.VMEM((4, 4, 2, 64, 1024), BF16),
            tokens(512),
            pltpu.VMEM((64, 1024), BF16),
            tokens(1536), tokens(512), tokens(512), tokens(512, F32), tokens(512, F32),
            pltpu.VMEM((4, 4, 64, 256), F32),
            pltpu.VMEM((4, 64, 256), F32),
            pltpu.VMEM((64, 16, 64), F32),
            pltpu.VMEM((16, 256), F32),
            pltpu.VMEM((2, 64, 256), F32),
            tokens(512), tokens(512), tokens(512, F32), tokens(512, F32), tokens(1536),
            tokens(512, F32), tokens(1, F32), tokens(512), tokens(512), tokens(512),
            tokens(512), tokens(512),
            pltpu.VMEM((1, 512), F32),
            tokens(512), tokens(256), tokens(512), tokens(256), tokens(512), tokens(256),
            pltpu.VMEM((64, 1024), BF16),
            pltpu.VMEM((64, 1024), BF16),
            tokens(512), tokens(1536),
            pltpu.VMEM((2, 4, 4, 32, 1024), BF16),
            pltpu.VMEM((2, 4, 4, 16, 1024), BF16),
            tokens(256),
            *[tokens(256) for _ in range(6)],
            pltpu.VMEM((512, 512), BF16),
            pltpu.VMEM((512, 512), BF16),
            tokens(256), tokens(256), tokens(128),
            *reduce_scratch(32, 64),
            *reduce_scratch(16, 32),
            sems((COPIES,)),
            sems((COPIES,)),
            sems((16,)),
        ],
        compiler_params=pltpu.CompilerParams(
            collective_id=0, has_side_effects=True, vmem_limit_bytes=60 * 1024 * 1024
        ),
        name="block_forward_backward",
    )(
        stash_values, scale_exp, cotangent, w_qkv, w_out, w_reduce,
        logit_scale.reshape(1, 16), bias_table.T, rel_index, norm_gain.reshape(1, 512), merge_gain.reshape(1, 1024),
        const(T_BLOCK), const(T_CBLOCK), const(WIN_ORDER), const(ROW_CUT, F32), const(COL_CUT, F32),
        const(T_MERGE), const(T_CMERGE), const(T_BLOCK.T), const(T_MERGE.T), const(T_CBLOCK.T), const(T_CMERGE.T),
        const(COLUMNS_64), const(COLUMNS_16),
        const(same_block(256, 64, 256, 64)), const(same_block(256, 32, 256, 32)), const(same_block(256, 64, 128, 32)),
    )
    return pl.pallas_call(
        hand_on,
        out_shape=outputs,
        in_specs=[vmem] * 5,
        out_specs=(vmem,) * 5,
        name="hand_on",
    )(*results)


def solution(mesh):
    tile = P("wide", "narrow", None)
    rows = P("wide", None)
    both = P("wide", "narrow")
    return jax.shard_map(
        on_device,
        mesh=mesh,
        in_specs=(tile, both, rows, rows, rows, P(), P(), P(), P(), P(), tile),
        out_specs=(tile, tile, both, both, both),
        check_vma=False,
    )
```

time: 636 us -> 83.1 us (0.13)
  waiting for transfers between devices: 435 us -> 0 us
  Pallas kernels: 0 us -> 82.3 us
  local copies, waits for them, and re-layouts: 63.3 us -> 0 us
  blocking collectives: 42.2 us -> 0 us
  matrix products: 40.8 us -> 0 us
  starting transfers between devices: 18.8 us -> 0 us
  other arithmetic: 14.8 us -> 0 us
  between operations: 15.1 us -> 0.64 us
    unnamed x11 -> x0, waiting for transfers between devices: 253 us -> none
    reduce_scatter x3 -> x0, waiting for transfers between devices: 145 us -> none  [the longest x1 88.6 us: on_device(): lax.psum_scatter(part_sums[2].astype(jnp.bfloat16), 'wide', scatter_dimen...]
    pallas_call x0 -> x2, Pallas kernels: none -> 82.3 us  [the longest x1 80.5 us: on_device(): pl.pallas_call(block_kernel, out_shape=outputs, in_specs=[vmem] * 16 + [p...]
    all_gather x1 -> x0, blocking collectives: 42.2 us -> none  [on_device(): lax.all_gather(w_out, 'wide', axis=0, tiled=True)]
    dot_general x16 -> x0, matrix products: 40.8 us -> none  [the longest x3 11.9 us: window_attention(): jnp.einsum('wihd,wjhd->whij', queries / query_norm, key_rows / key_norm,...]
    ppermute x8 -> x0, waiting for transfers between devices: 31 us -> none  [from_behind(): return lax.ppermute(block, axis, route)]
    unnamed x91 -> x0, local copies, waits for them, and re-layouts: 19.3 us -> none
    ppermute x8 -> x0, starting transfers between devices: 18 us -> none  [from_behind(): return lax.ppermute(block, axis, route)]
  transfers between devices with their start and end apart: 16 -> 0, of which waited for: 14 -> 0; matrix products, arithmetic and copies ran while one was open for 14% -> 0% of each run, Pallas kernels for 0% -> 0%
where the time goes in v1:
time: 83.1 us; the launch traced here: 83 us
  Pallas kernels  82.3 us (99%)
    pallas_call x1, Pallas kernels, on_device(): pl.pallas_call(block_kernel, out_shape=outputs, in_specs=[vmem] * 16 + [p...  80.5 us
    pallas_call x1, Pallas kernels, on_device(): pl.pallas_call(hand_on, out_shape=outputs, in_specs=[vmem] * 5, out_specs...  1.78 us

profile of v1, /device:TPU:2, one launch (start us, length us, event | category | flops | bytes accessed | tf_op | source)
XLA Modules:
  0.0 83.0 jit_solution(8934954756029145973)
XLA Ops:
  0.6 80.5 %block_forward_backward.1 = (bf16[4,16,1024]{2,1,0:T(8,128)(2,1)}, bf16[8,32,512]{2,1,0:T(8,128)(2,1)}, f32[16,192]{1,0:T(8,128)}, f32[16,64]{1,0:T(8,128)}, f32[64,128]{1,0:T(8,128)}) custom-call(s32[8,32,512]{2,1,0:T(8,128)} %stash_ref.1, s32[1,4]{1,0:T(1,128)} %exp_ref.1, bf16[4,16,1024]{2,1,0:T(8,128)(2,1)} %cot_ref.1, bf16[16,1536]{1,0:T(8,128)(2,1)} %wq_ref.1, ...), custom_call_target="tpu_custom_call" | custom-call | tf_op jit(solution)/shard_map/block_forward_backward/pallas_call | solution.py:730
  81.2 1.8 %hand_on.1 = (bf16[4,16,1024]{2,1,0:T(8,128)(2,1)}, bf16[8,32,512]{2,1,0:T(8,128)(2,1)}, f32[16,192]{1,0:T(8,128)}, f32[16,64]{1,0:T(8,128)}, f32[64,128]{1,0:T(8,128)}) custom-call(bf16[4,16,1024]{2,1,0:T(8,128)(2,1)} %get-tuple-element.10.refs_0_, bf16[8,32,512]{2,1,0:T(8,128)(2,1)} %get-tuple-element.11.refs_1_, f32[16,192]{1,0:T(8,128)} %get-tuple-element.12.refs_2_, ...), custom_call_target="tpu_custom_call" | custom-call | tf_op jit(solution)/shard_map/hand_on/pallas_call | solution.py:781

commit v2 on v1

--- a/solution.py
+++ b/solution.py
@@ -127,7 +127,10 @@
     barrier = pltpu.get_barrier_semaphore()
     for device in devices:
         pl.semaphore_signal(barrier, inc=1, device_id=device, device_id_type=MESH)
-    pl.semaphore_wait(barrier, len(devices))
+
+
+def wait_for(devices):
+    pl.semaphore_wait(pltpu.get_barrier_semaphore(), len(devices))
 
 
 def lanes(start, size):
@@ -219,6 +222,11 @@
             self.share(self.x_right, EVERY)
 
     def x3(self):
+        if self.direct and not self.quarters:
+            for copy, x in zip(self.x, (self.x_left, self.x_far, self.x_right)):
+                copy.wait_recv()
+                self.share(x, EVERY)
+            return
         for copy in self.x:
             copy.wait_recv()
         if not self.quarters:
@@ -263,6 +271,7 @@
         self.zsend, self.zland = zsend, zland
         self.xs = [lax.rem(at.x + step, 4) for step in (2, 1, 3, 0)]
         self.ys = [lax.rem(at.y + step, 4) for step in (2, 1, 3, 0)]
+        self.d = []
         self.x_left, self.x_right = at.at_x(-1), at.at_x(1)
         self.y_left, self.y_right = at.at_y(-1), at.at_y(1)
 
@@ -311,7 +320,6 @@
             copy.wait_recv()
         for s in range(4):
             self.cx[s] = add(self.m[0, at.x, s], self.bx2[0, s], self.bx2[1, s]).astype(BF16)
-        self.d = []
         for n, step in ((0, 2), (1, 1), (2, 3)):
             src = self.cx.at[:, :, y_cut(self.ys[n])]
             self.d.append(self.go.remote(src, self.dx.at[n], at.at_y(step)))
@@ -382,45 +390,55 @@
 
 
 def block_kernel(
-    stash_ref, exp_ref, cot_ref, wq_ref, wo_ref, wr_ref, ls_ref, table_ref, rel_ref, ng_ref, mg_ref,
-    t_block_ref, t_cblock_ref, order_ref, row_cut_ref, col_cut_ref, *rest,
+    wq_ref, wo_ref, wr_ref, *rest,
 ):
-    tables, rest = rest[:11], rest[11:]
+    loads, rest = rest[:24], rest[24:]
     (
     merged_ref, gin_ref, gq_ref, go_ref, gr_ref,
     blk, land, back, oland, ocland, wq, wo, wr,
     x_tok, cot_tok, qkv, qs, kh, rq, rk, probs, bias, bias_rows, table, mask, att, d_att, dqs, dkh, dqkv,
     xhat, xscale, ro, dproj, dtok, xt, at_t, ls_row, ro_cols, ro_theirs, x_cols, x_theirs, at_cols, at_theirs,
     dred, dred_theirs, dproj_theirs, dqkv_theirs, fa, fb, mb,
-    t_merge_ref, t_cmerge_ref, t_unblock_ref, t_unmerge_ref, t_cunblock_ref, t_cunmerge_ref,
-    columns_ref, columns_16_ref, bd64_ref, bd32_ref, heads_ref,
     *rest,
     ) = rest
+    held, rest = rest[:24], rest[24:]
+    (
+        stash_ref, exp_ref, t_block_ref, cot_ref, t_cblock_ref,
+        table_ref, rel_ref, order_ref, row_cut_ref, col_cut_ref, ls_ref,
+        ng_ref, mg_ref, t_merge_ref, t_cmerge_ref, t_unblock_ref, t_unmerge_ref, t_cunblock_ref, t_cunmerge_ref,
+        columns_ref, columns_16_ref, bd64_ref, bd32_ref, heads_ref,
+    ) = held
     a_bufs, b_bufs, (send_sem, recv_sem, local_sem) = rest[0:10], rest[10:20], rest[20:]
-    held = (
-        t_merge_ref, t_cmerge_ref, t_unblock_ref, t_unmerge_ref, t_cunblock_ref, t_cunmerge_ref,
-        columns_ref, columns_16_ref, bd64_ref, bd32_ref, heads_ref,
-    )
     go = Sender(send_sem, recv_sem, local_sem)
-    table_copies = [go.local(src, dst) for src, dst in zip(tables, held)]
     at = Place()
     c = at.core
-    greet(
+    partners = (
         [at.sibling]
         + [at.at_x(step) for step in (1, 2, 3)]
         + [at.at_y(step) for step in (1, 2, 3)]
         + [at.at_z(step) for step in range(1, 8)]
         + [at.at_tile(*step) for step in ((-1, 0), (0, -1), (-1, -1), (1, 0), (0, 1), (1, 1))]
     )
+    greet(partners)
+    arrivals = [go.local(src, dst) for src, dst in zip(loads, held)]
+
+    def loaded(first, last):
+        for copy in arrivals[first:last]:
+            copy.wait()
+
+    wait_for(partners)
     all_rows = pl.ds(0, 16)
     q_y = Gather(at, go, wq_ref, wq, lambda y: (all_rows, lanes(512 + 256 * y, 256)), True, True)
-    q_x = Gather(at, go, wq_ref, wq, lambda y: (all_rows, pl.ds(0, 512)))
+    q_x = Gather(at, go, wq_ref, wq, lambda y: (all_rows, pl.ds(0, 512)), False, True)
     o_x = Gather(at, go, wo_ref, wo, lambda y: (all_rows, pl.ds(0, 512)))
     r_x = Gather(at, go, wr_ref, wr, lambda y: (pl.ds(0, 64), pl.ds(0, 512)))
     r_y = Gather(at, go, wr_ref, wr, lambda y: (pl.ds(pl.multiple_of(16 * y, 16), 16), pl.ds(512, 512)), True)
 
     q_y.start()
-
+    r_y.start()
+    q_x.start()
+
+    loaded(0, 5)
     factor_of = exp_ref[...]
     factor_of = jnp.where(factor_of == -8, 2.0**-8, jnp.where(factor_of == -7, 2.0**-7, 2.0**-6))
     in_window = lax.broadcasted_iota(jnp.int32, (32, 512), 0) // 8
@@ -429,19 +447,23 @@
         factor = jnp.where(in_window == w, factor_of[:, w : w + 1], factor)
     inputs = stash_ref[...].astype(F32) * factor[None]
     blk[:, 0:512] = mm(t_block_ref[...], inputs.reshape(256, 512).astype(BF16)).astype(BF16)
-    r_y.start()
+    r_x.start()
+    q_y.x1()
+    r_y.x1()
+    o_x.start()
+    q_x.x1()
     cot = cot_ref[...].astype(F32).reshape(64, 1024).astype(BF16)
     cot = jnp.concatenate([cot[:, 256 * q : 256 * q + 256] for q in range(4)], 0)
     blk[:, 512:768] = mm(t_cblock_ref[...], cot).astype(BF16)
-    q_x.start()
-    q_y.x1()
-    r_x.start()
-    r_y.x1()
-    q_x.x1()
-    o_x.start()
     q_y.y1()
-    q_x.x2()
-
+    halo = [
+        go.remote(blk.at[pl.ds(16, 112)], land.at[pl.ds(128, 112)], at.at_tile(-1, 0)),
+        go.remote(blk.at[pl.ds(128, 16)], land.at[pl.ds(112, 16)], at.at_tile(0, -1)),
+        go.remote(blk.at[pl.ds(0, 16)], land.at[pl.ds(240, 16)], at.at_tile(-1, -1)),
+    ]
+    r_y.x2()
+
+    loaded(5, 11)
     table[...] = jnp.zeros((16, 256), F32)
     table[:, 0:225] = 16.0 * jax.nn.sigmoid(table_ref[...])
     by_head = table[...]
@@ -462,20 +484,13 @@
                 bias_rows[16 * j + a] = got[:, 64 * j : 64 * j + 64]
 
     bias_of(range(0, 5))
-    r_y.x2()
-    halo = [
-        go.remote(blk.at[pl.ds(16, 112)], land.at[pl.ds(128, 112)], at.at_tile(-1, 0)),
-        go.remote(blk.at[pl.ds(128, 16)], land.at[pl.ds(112, 16)], at.at_tile(0, -1)),
-        go.remote(blk.at[pl.ds(0, 16)], land.at[pl.ds(240, 16)], at.at_tile(-1, -1)),
-    ]
     r_x.x1()
     bias_of(range(5, 10))
     q_y.y2()
-    q_x.x3()
     r_y.y1()
     bias_of(range(10, 16))
     o_x.x1()
-    q_y.y3()
+    q_x.x3()
     for g in range(4):
         bias[g] = jnp.concatenate([bias_rows[:, 4 * g + h, :] for h in range(4)], 1)
     last_rows = (at.wide == 31).astype(F32)
@@ -489,27 +504,27 @@
     ls_row[...] = scales
 
 
+    q_y.y3()
+    q_x.done()
+
     for copy in halo:
         copy.wait_recv()
-    for copy in table_copies:
-        copy.wait()
     r_x.x2()
+    loaded(11, 24)
+    q_y.done()
     land[pl.ds(0, 112)] = blk[pl.ds(144, 112)]
     x_tok[...] = mm(t_merge_ref[...], land[:, 0:512]).astype(BF16)
     cot = mm(t_cmerge_ref[...], land[:, 512:768]).astype(BF16)
     cot_tok[...] = jnp.concatenate([cot[64 * q : 64 * q + 64] for q in range(4)], 1)
+    r_y.y2()
+    o_x.x2()
     x_cols[...] = mm(x_tok[...], columns_16_ref[...]).astype(BF16)
     not_mine = lanes(256 * (1 - c), 256)
     mine = lanes(256 * c, 256)
     x_swap = go.remote(x_cols.at[:, not_mine], x_theirs, at.sibling)
-    q_x.done()
-    o_x.x2()
-    q_y.done()
-    r_y.y2()
 
     qkv[...] = mm(x_tok[...], wq[...].reshape(512, 1536)).astype(BF16)
     r_x.x3()
-    o_x.x3()
     for start, inverse, unit in ((0, rq, qs), (512, rk, kh)):
         for n in range(2):
             cut = slice(256 * n, 256 * n + 256)
@@ -556,6 +571,7 @@
 
     forward(0)
     forward(1)
+    o_x.x3()
     r_y.y3()
     forward(2)
     forward(3)
@@ -609,19 +625,13 @@
         if n == 0:
             a_sum.first_x()
     a_sum.first_y()
-    merged_back = send_back(mb, ocland)
 
     for row in range(0, 256, 64):
         rows = slice(row, row + 64)
         got = norm_back(dtok[rows].astype(F32), xhat[rows], xscale[rows], ng_ref[...])
         dproj[rows] = got.astype(BF16)
     dproj_swap = go.remote(dproj, dproj_theirs, at.sibling)
-    a_sum.second_x()
-    at_swap.wait_recv()
-    at_t[:, 0:256] = at_cols[:, mine].T
-    at_t[:, 256:512] = at_theirs[...].T
     d_att[...] = dg(dproj[...], wo[...].reshape(512, 512), NT).astype(BF16)
-    a_sum.second_y()
 
     def backward(g):
         cut = slice(g * 128, g * 128 + 128)
@@ -646,6 +656,8 @@
         return go.remote(dqkv.at[:, cut], dqkv_theirs.at[:, cut], at.sibling)
 
     dqkv_swap = [swap_dqkv(1024)]
+    a_sum.second_x()
+    a_sum.second_y()
     for start, inverse, grad in ((0, rq, dqs), (512, rk, dkh)):
         for n in range(2):
             cut = slice(256 * n, 256 * n + 256)
@@ -661,12 +673,19 @@
                 along = jnp.where(inv < 1e12, along, 0.0)
                 dqkv[rows, both_cut] = (inv * (d_unit - unit * along)).astype(BF16)
         dqkv_swap.append(swap_dqkv(start))
-    a_sum.third_x()
+    at_swap.wait_recv()
+    at_t[:, 0:256] = at_cols[:, mine].T
+    at_t[:, 256:512] = at_theirs[...].T
     dproj_swap.wait_recv()
     d_out = jnp.concatenate([dproj[...], dproj_theirs[...]], 0)
     out = mm(at_t[...], d_out).astype(BF16)
     for y in range(4):
         fb[1, :, :, :, 256 * y + 128 : 256 * y + 256] = out[:, 128 * y : 128 * y + 128].reshape(4, 4, 16, 128)
+
+    merged_back = send_back(mb, ocland)
+    d_in = dtok[...].astype(F32) + dg(dqkv[...], wq[...].reshape(512, 1536), NT)
+    back[...] = mm(t_unmerge_ref[...], d_in.astype(BF16)).astype(BF16)
+    grad_back = send_back(back, oland)
 
     for copy in dqkv_swap:
         copy.wait_recv()
@@ -680,26 +699,22 @@
         fb[1, :, :, :, lanes(256 * y, 128)] = got[:, 256:384].reshape(4, 4, 16, 128)
     b_sum.first_x()
     b_sum.first_y()
+    a_sum.third_x()
     a_sum.third_y()
-    d_in = dtok[...].astype(F32) + dg(dqkv[...], wq[...].reshape(512, 1536), NT)
-    back[...] = mm(t_unmerge_ref[...], d_in.astype(BF16)).astype(BF16)
-    grad_back = send_back(back, oland)
+    b_sum.second_y()
     b_sum.second_x()
-    b_sum.second_y()
     a_sum.fourth(pack_reduce)
-    for copy in grad_back:
+    b_sum.third_y()
+    b_sum.third_x()
+    b_sum.fourth(pack_qkv_out)
+    for copy in merged_back + grad_back:
         copy.wait_recv()
     oland[pl.ds(144, 112)] = back[pl.ds(0, 112)]
-    b_sum.third_x()
-    b_sum.third_y()
-    b_sum.fourth(pack_qkv_out)
-    for copy in merged_back:
-        copy.wait_recv()
     ocland[pl.ds(144, 112)] = mb[pl.ds(0, 112)]
+    gin_ref[...] = mm(t_unblock_ref[...], oland[...]).astype(BF16).reshape(8, 32, 512)
     got = mm(t_cunblock_ref[...], ocland[...]).astype(BF16)
     for q in range(4):
         merged_ref[:, :, 256 * q : 256 * q + 256] = got[64 * q : 64 * q + 64].reshape(4, 16, 256)
-    gin_ref[...] = mm(t_unblock_ref[...], oland[...]).astype(BF16).reshape(8, 32, 512)
     factor = 1.0 / 256.0
     gr_ref[...] = a_sum.fifth() * factor
     go.drain()
@@ -726,11 +741,19 @@
         jax.ShapeDtypeStruct((16, 64), F32),
         jax.ShapeDtypeStruct((64, 128), F32),
     )
+    loads = (
+        stash_values, scale_exp, const(T_BLOCK), cotangent, const(T_CBLOCK),
+        bias_table.T, rel_index, const(WIN_ORDER), const(ROW_CUT, F32), const(COL_CUT, F32), logit_scale.reshape(1, 16),
+        norm_gain.reshape(1, 512), merge_gain.reshape(1, 1024),
+        const(T_MERGE), const(T_CMERGE), const(T_BLOCK.T), const(T_MERGE.T), const(T_CBLOCK.T), const(T_CMERGE.T),
+        const(COLUMNS_64), const(COLUMNS_16),
+        const(same_block(256, 64, 256, 64)), const(same_block(256, 32, 256, 32)), const(same_block(256, 64, 128, 32)),
+    )
     tokens = lambda width, kind=BF16: pltpu.VMEM((256, width), kind)
     results = pl.pallas_call(
         block_kernel,
         out_shape=outputs,
-        in_specs=[vmem] * 16 + [pl.BlockSpec(memory_space=pl.ANY)] * 11,
+        in_specs=[pl.BlockSpec(memory_space=pl.ANY)] * 27,
         out_specs=(vmem,) * 5,
         scratch_shapes=[
             tokens(768), tokens(768), tokens(512), tokens(512), tokens(256),
@@ -756,28 +779,18 @@
             pltpu.VMEM((2, 4, 4, 32, 1024), BF16),
             pltpu.VMEM((2, 4, 4, 16, 1024), BF16),
             tokens(256),
-            *[tokens(256) for _ in range(6)],
-            pltpu.VMEM((512, 512), BF16),
-            pltpu.VMEM((512, 512), BF16),
-            tokens(256), tokens(256), tokens(128),
+            *[pltpu.VMEM(load.shape, load.dtype) for load in loads],
             *reduce_scratch(32, 64),
             *reduce_scratch(16, 32),
             sems((COPIES,)),
             sems((COPIES,)),
-            sems((16,)),
+            sems((32,)),
         ],
         compiler_params=pltpu.CompilerParams(
             collective_id=0, has_side_effects=True, vmem_limit_bytes=60 * 1024 * 1024
         ),
         name="block_forward_backward",
-    )(
-        stash_values, scale_exp, cotangent, w_qkv, w_out, w_reduce,
-        logit_scale.reshape(1, 16), bias_table.T, rel_index, norm_gain.reshape(1, 512), merge_gain.reshape(1, 1024),
-        const(T_BLOCK), const(T_CBLOCK), const(WIN_ORDER), const(ROW_CUT, F32), const(COL_CUT, F32),
-        const(T_MERGE), const(T_CMERGE), const(T_BLOCK.T), const(T_MERGE.T), const(T_CBLOCK.T), const(T_CMERGE.T),
-        const(COLUMNS_64), const(COLUMNS_16),
-        const(same_block(256, 64, 256, 64)), const(same_block(256, 32, 256, 32)), const(same_block(256, 64, 128, 32)),
-    )
+    )(w_qkv, w_out, w_reduce, *loads)
     return pl.pallas_call(
         hand_on,
         out_shape=outputs,

time: 83.1 us -> 79.3 us (0.954)
  Pallas kernels: 82.3 us -> 78.2 us
    pallas_call x1, Pallas kernels: 80.5 us -> 76.4 us  [on_device(): pl.pallas_call(block_kernel, out_shape=outputs, in_specs=[pl.BlockSpec(me...]
where the time goes in v2:
time: 79.3 us; the launch traced here: 78.8 us
  Pallas kernels  78.2 us (99%)
    pallas_call x1, Pallas kernels, on_device(): pl.pallas_call(block_kernel, out_shape=outputs, in_specs=[pl.BlockSpec(me...  76.4 us
    pallas_call x1, Pallas kernels, on_device(): pl.pallas_call(hand_on, out_shape=outputs, in_specs=[vmem] * 5, out_specs...  1.78 us

profile of v2, /device:TPU:2, one launch (start us, length us, event | category | flops | bytes accessed | tf_op | source)
XLA Modules:
  0.0 78.8 jit_solution(7391142351424876949)
XLA Ops:
  0.6 76.4 %block_forward_backward.1 = (bf16[4,16,1024]{2,1,0:T(8,128)(2,1)}, bf16[8,32,512]{2,1,0:T(8,128)(2,1)}, f32[16,192]{1,0:T(8,128)}, f32[16,64]{1,0:T(8,128)}, f32[64,128]{1,0:T(8,128)}) custom-call(bf16[16,1536]{1,0:T(8,128)(2,1)} %wq_ref.1, bf16[16,512]{1,0:T(8,128)(2,1)} %wo_ref.1, bf16[64,1024]{1,0:T(8,128)(2,1)} %wr_ref.1, s32[8,32,512]{2,1,0:T(8,128)} %rest_0_.1, ...), custom_call_target="tpu_custom_call" | custom-call | tf_op jit(solution)/shard_map/block_forward_backward/pallas_call | solution.py:753
  77.1 1.8 %hand_on.1 = (bf16[4,16,1024]{2,1,0:T(8,128)(2,1)}, bf16[8,32,512]{2,1,0:T(8,128)(2,1)}, f32[16,192]{1,0:T(8,128)}, f32[16,64]{1,0:T(8,128)}, f32[64,128]{1,0:T(8,128)}) custom-call(bf16[4,16,1024]{2,1,0:T(8,128)(2,1)} %get-tuple-element.10.refs_0_, bf16[8,32,512]{2,1,0:T(8,128)(2,1)} %get-tuple-element.11.refs_1_, f32[16,192]{1,0:T(8,128)} %get-tuple-element.12.refs_2_, ...), custom_call_target="tpu_custom_call" | custom-call | tf_op jit(solution)/shard_map/hand_on/pallas_call | solution.py:794

commit v3 on v2

--- a/solution.py
+++ b/solution.py
@@ -95,7 +95,7 @@
 class Sender:
     def __init__(self, send_sem, recv_sem, local_sem):
         self.send_sem, self.recv_sem, self.local_sem = send_sem, recv_sem, local_sem
-        self.started, self.count, self.local_count = [], 0, 0
+        self.started, self.count, self.local_count, self.drained = [], 0, 0, 0
 
     def remote(self, src, dst, device):
         copy = pltpu.make_async_remote_copy(
@@ -117,10 +117,11 @@
         copy.start()
         return copy
 
-    def drain(self):
-        for copy in self.started:
+    def drain(self, until=None):
+        until = self.count if until is None else until
+        for copy in self.started[self.drained : until]:
             copy.wait_send()
-        self.started = []
+        self.drained = until
 
 
 def greet(devices):
@@ -429,41 +430,15 @@
     wait_for(partners)
     all_rows = pl.ds(0, 16)
     q_y = Gather(at, go, wq_ref, wq, lambda y: (all_rows, lanes(512 + 256 * y, 256)), True, True)
-    q_x = Gather(at, go, wq_ref, wq, lambda y: (all_rows, pl.ds(0, 512)), False, True)
+    q_x = Gather(at, go, wq_ref, wq, lambda y: (all_rows, pl.ds(0, 512)))
     o_x = Gather(at, go, wo_ref, wo, lambda y: (all_rows, pl.ds(0, 512)))
     r_x = Gather(at, go, wr_ref, wr, lambda y: (pl.ds(0, 64), pl.ds(0, 512)))
-    r_y = Gather(at, go, wr_ref, wr, lambda y: (pl.ds(pl.multiple_of(16 * y, 16), 16), pl.ds(512, 512)), True)
+    r_y = Gather(at, go, wr_ref, wr, lambda y: (pl.ds(pl.multiple_of(16 * y, 16), 16), pl.ds(512, 512)), True, True)
 
     q_y.start()
     r_y.start()
-    q_x.start()
-
-    loaded(0, 5)
-    factor_of = exp_ref[...]
-    factor_of = jnp.where(factor_of == -8, 2.0**-8, jnp.where(factor_of == -7, 2.0**-7, 2.0**-6))
-    in_window = lax.broadcasted_iota(jnp.int32, (32, 512), 0) // 8
-    factor = jnp.zeros((32, 512), F32)
-    for w in range(4):
-        factor = jnp.where(in_window == w, factor_of[:, w : w + 1], factor)
-    inputs = stash_ref[...].astype(F32) * factor[None]
-    blk[:, 0:512] = mm(t_block_ref[...], inputs.reshape(256, 512).astype(BF16)).astype(BF16)
-    r_x.start()
-    q_y.x1()
-    r_y.x1()
-    o_x.start()
-    q_x.x1()
-    cot = cot_ref[...].astype(F32).reshape(64, 1024).astype(BF16)
-    cot = jnp.concatenate([cot[:, 256 * q : 256 * q + 256] for q in range(4)], 0)
-    blk[:, 512:768] = mm(t_cblock_ref[...], cot).astype(BF16)
-    q_y.y1()
-    halo = [
-        go.remote(blk.at[pl.ds(16, 112)], land.at[pl.ds(128, 112)], at.at_tile(-1, 0)),
-        go.remote(blk.at[pl.ds(128, 16)], land.at[pl.ds(112, 16)], at.at_tile(0, -1)),
-        go.remote(blk.at[pl.ds(0, 16)], land.at[pl.ds(240, 16)], at.at_tile(-1, -1)),
-    ]
-    r_y.x2()
-
-    loaded(5, 11)
+
+    loaded(0, 11)
     table[...] = jnp.zeros((16, 256), F32)
     table[:, 0:225] = 16.0 * jax.nn.sigmoid(table_ref[...])
     by_head = table[...]
@@ -484,13 +459,39 @@
                 bias_rows[16 * j + a] = got[:, 64 * j : 64 * j + 64]
 
     bias_of(range(0, 5))
+    o_x.start()
+
+    factor_of = exp_ref[...]
+    factor_of = jnp.where(factor_of == -8, 2.0**-8, jnp.where(factor_of == -7, 2.0**-7, 2.0**-6))
+    in_window = lax.broadcasted_iota(jnp.int32, (32, 512), 0) // 8
+    factor = jnp.zeros((32, 512), F32)
+    for w in range(4):
+        factor = jnp.where(in_window == w, factor_of[:, w : w + 1], factor)
+    inputs = stash_ref[...].astype(F32) * factor[None]
+    blk[:, 0:512] = mm(t_block_ref[...], inputs.reshape(256, 512).astype(BF16)).astype(BF16)
+    q_x.start()
+    q_y.x1()
+    cot = cot_ref[...].astype(F32).reshape(64, 1024).astype(BF16)
+    cot = jnp.concatenate([cot[:, 256 * q : 256 * q + 256] for q in range(4)], 0)
+    blk[:, 512:768] = mm(t_cblock_ref[...], cot).astype(BF16)
+    r_y.x1()
+    r_x.start()
+    q_x.x1()
+    q_y.y1()
+    o_x.x1()
+    halo = [
+        go.remote(blk.at[pl.ds(16, 112)], land.at[pl.ds(128, 112)], at.at_tile(-1, 0)),
+        go.remote(blk.at[pl.ds(128, 16)], land.at[pl.ds(112, 16)], at.at_tile(0, -1)),
+        go.remote(blk.at[pl.ds(0, 16)], land.at[pl.ds(240, 16)], at.at_tile(-1, -1)),
+    ]
+    bias_of(range(5, 10))
+    r_y.y1()
+    q_x.x2()
     r_x.x1()
-    bias_of(range(5, 10))
+    bias_of(range(10, 16))
     q_y.y2()
-    r_y.y1()
-    bias_of(range(10, 16))
-    o_x.x1()
     q_x.x3()
+    o_x.x2()
     for g in range(4):
         bias[g] = jnp.concatenate([bias_rows[:, 4 * g + h, :] for h in range(4)], 1)
     last_rows = (at.wide == 31).astype(F32)
@@ -504,26 +505,28 @@
     ls_row[...] = scales
 
 
-    q_y.y3()
-    q_x.done()
-
     for copy in halo:
         copy.wait_recv()
+    r_y.y2()
+    q_y.y3()
     r_x.x2()
+    o_x.x3()
     loaded(11, 24)
-    q_y.done()
     land[pl.ds(0, 112)] = blk[pl.ds(144, 112)]
     x_tok[...] = mm(t_merge_ref[...], land[:, 0:512]).astype(BF16)
     cot = mm(t_cmerge_ref[...], land[:, 512:768]).astype(BF16)
     cot_tok[...] = jnp.concatenate([cot[64 * q : 64 * q + 64] for q in range(4)], 1)
-    r_y.y2()
-    o_x.x2()
     x_cols[...] = mm(x_tok[...], columns_16_ref[...]).astype(BF16)
     not_mine = lanes(256 * (1 - c), 256)
     mine = lanes(256 * c, 256)
     x_swap = go.remote(x_cols.at[:, not_mine], x_theirs, at.sibling)
 
+    q_x.done()
+    q_y.done()
+
     qkv[...] = mm(x_tok[...], wq[...].reshape(512, 1536)).astype(BF16)
+    r_y.y3()
+    o_x.done()
     r_x.x3()
     for start, inverse, unit in ((0, rq, qs), (512, rk, kh)):
         for n in range(2):
@@ -569,16 +572,11 @@
             values = spread(window(qkv, win, v_cut))
             put_window(att, win, cut, mm(p.astype(BF16), values).astype(BF16))
 
-    forward(0)
-    forward(1)
-    o_x.x3()
-    r_y.y3()
-    forward(2)
-    forward(3)
-    r_x.done()
+    for g in range(4):
+        forward(g)
     at_cols[...] = mm(att[...], columns_16_ref[...]).astype(BF16)
     at_swap = go.remote(at_cols.at[:, not_mine], at_theirs, at.sibling)
-    o_x.done()
+    r_y.done()
     xhat[...] = mm(att[...], wo[...].reshape(512, 512))
     for row in range(0, 256, 64):
         rows = slice(row, row + 64)
@@ -588,7 +586,7 @@
         ro[rows] = (x_tok[rows].astype(F32) + normed * ng_ref[...]).astype(BF16)
     ro_cols[...] = mm(ro[...], columns_ref[...]).astype(BF16)
     swap = [go.remote(ro_cols.at[:, not_mine], ro_theirs, at.sibling)]
-    r_y.done()
+    r_x.done()
 
     reduced = jnp.zeros((64, 1024), F32)
     for k in range(4):
@@ -610,8 +608,16 @@
     for k in range(4):
         dtok[64 * k : 64 * k + 64] = dg(dred[...], wr[k].reshape(512, 1024), NT).astype(BF16)
 
+    for row in range(0, 256, 64):
+        rows = slice(row, row + 64)
+        got = norm_back(dtok[rows].astype(F32), xhat[rows], xscale[rows], ng_ref[...])
+        dproj[rows] = got.astype(BF16)
+    dproj_swap = go.remote(dproj, dproj_theirs, at.sibling)
+    d_att[...] = dg(dproj[...], wo[...].reshape(512, 512), NT).astype(BF16)
+
     for copy in swap:
         copy.wait_recv()
+    before_a = go.count
     a_sum = Reduce(at, go, fa, *a_bufs)
     grads = jnp.concatenate([dred[...], dred_theirs[...]], 0)
     for n in range(4):
@@ -625,13 +631,6 @@
         if n == 0:
             a_sum.first_x()
     a_sum.first_y()
-
-    for row in range(0, 256, 64):
-        rows = slice(row, row + 64)
-        got = norm_back(dtok[rows].astype(F32), xhat[rows], xscale[rows], ng_ref[...])
-        dproj[rows] = got.astype(BF16)
-    dproj_swap = go.remote(dproj, dproj_theirs, at.sibling)
-    d_att[...] = dg(dproj[...], wo[...].reshape(512, 512), NT).astype(BF16)
 
     def backward(g):
         cut = slice(g * 128, g * 128 + 128)
@@ -689,6 +688,7 @@
 
     for copy in dqkv_swap:
         copy.wait_recv()
+    before_b = go.count
     b_sum = Reduce(at, go, fb, *b_bufs)
     for n in range(4):
         y = b_sum.ys[n]
@@ -699,14 +699,18 @@
         fb[1, :, :, :, lanes(256 * y, 128)] = got[:, 256:384].reshape(4, 4, 16, 128)
     b_sum.first_x()
     b_sum.first_y()
+    go.drain(before_a // 2)
     a_sum.third_x()
     a_sum.third_y()
     b_sum.second_y()
     b_sum.second_x()
+    go.drain(before_b)
+    before_c = go.count
     a_sum.fourth(pack_reduce)
     b_sum.third_y()
     b_sum.third_x()
     b_sum.fourth(pack_qkv_out)
+    go.drain(before_c)
     for copy in merged_back + grad_back:
         copy.wait_recv()
     oland[pl.ds(144, 112)] = back[pl.ds(0, 112)]

time: 79.3 us -> 79.3 us (level)
  no operation moved by 1% of the time
where the time goes in v3:
time: 79.3 us; the launch traced here: 78.8 us
  Pallas kernels  78.2 us (99%)
    pallas_call x1, Pallas kernels, on_device(): pl.pallas_call(block_kernel, out_shape=outputs, in_specs=[pl.BlockSpec(me...  76.4 us
    pallas_call x1, Pallas kernels, on_device(): pl.pallas_call(hand_on, out_shape=outputs, in_specs=[vmem] * 5, out_specs...  1.78 us

profile of v3, /device:TPU:2, one launch (start us, length us, event | category | flops | bytes accessed | tf_op | source)
XLA Modules:
  0.0 78.8 jit_solution(16267435275137286189)
XLA Ops:
  0.6 76.4 %block_forward_backward.1 = (bf16[4,16,1024]{2,1,0:T(8,128)(2,1)}, bf16[8,32,512]{2,1,0:T(8,128)(2,1)}, f32[16,192]{1,0:T(8,128)}, f32[16,64]{1,0:T(8,128)}, f32[64,128]{1,0:T(8,128)}) custom-call(bf16[16,1536]{1,0:T(8,128)(2,1)} %wq_ref.1, bf16[16,512]{1,0:T(8,128)(2,1)} %wo_ref.1, bf16[64,1024]{1,0:T(8,128)(2,1)} %wr_ref.1, s32[8,32,512]{2,1,0:T(8,128)} %rest_0_.1, ...), custom_call_target="tpu_custom_call" | custom-call | tf_op jit(solution)/shard_map/block_forward_backward/pallas_call | solution.py:757
  77.0 1.8 %hand_on.1 = (bf16[4,16,1024]{2,1,0:T(8,128)(2,1)}, bf16[8,32,512]{2,1,0:T(8,128)(2,1)}, f32[16,192]{1,0:T(8,128)}, f32[16,64]{1,0:T(8,128)}, f32[64,128]{1,0:T(8,128)}) custom-call(bf16[4,16,1024]{2,1,0:T(8,128)(2,1)} %get-tuple-element.10.refs_0_, bf16[8,32,512]{2,1,0:T(8,128)(2,1)} %get-tuple-element.11.refs_1_, f32[16,192]{1,0:T(8,128)} %get-tuple-element.12.refs_2_, ...), custom_call_target="tpu_custom_call" | custom-call | tf_op jit(solution)/shard_map/hand_on/pallas_call | solution.py:798

commit v4 on v3

--- a/solution.py
+++ b/solution.py
@@ -356,6 +356,77 @@
         return total
 
 
+class ReduceZ:
+    def __init__(self, at, go, m, r1, r2, r3, r4, ex, dx, ey, dy):
+        self.at, self.go, self.m = at, go, m
+        self.r1, self.rings = r1, (r2, r3, r4)
+        self.ex, self.dx, self.ey, self.dy = ex, dx, ey, dy
+
+    def slot(self, step):
+        z = lax.rem(self.at.z + step, 8)
+        return lax.div(z, 2), lax.rem(z, 2)
+
+    def first(self):
+        far = self.m.at[self.slot(4)]
+        self.sent = [
+            self.go.remote(far.at[pl.ds(0, 2)], self.r1.at[0], self.at.at_z(1)),
+            self.go.remote(far.at[pl.ds(2, 2)], self.r1.at[1], self.at.at_z(-1)),
+        ]
+
+    def step(self, n):
+        up, down = self.slot(4 - n), self.slot(4 + n)
+        for copy in self.sent:
+            copy.wait_recv()
+        for k in range(2 if n == 1 else 4):
+            if n == 1:
+                got, ups, downs = self.r1, up + (k,), down + (2 + k,)
+            else:
+                got, ups, downs = self.rings[n - 2], up + (k,), down + (k,)
+            self.m[ups] = add(self.m[ups], got[0, k]).astype(BF16)
+            self.m[downs] = add(self.m[downs], got[1, k]).astype(BF16)
+        self.sent = [
+            self.go.remote(self.m.at[up], self.rings[n - 1].at[0], self.at.at_z(1)),
+            self.go.remote(self.m.at[down], self.rings[n - 1].at[1], self.at.at_z(-1)),
+        ]
+
+    def fifth(self):
+        for copy in self.sent:
+            copy.wait_recv()
+        mine, last = self.slot(0), self.rings[2]
+        for k in range(4):
+            self.ex[k] = add(self.m[mine + (k,)], last[0, k], last[1, k]).astype(BF16)
+        self.sent = []
+        for n, step in enumerate((2, 1, 3)):
+            src = self.ex.at[lax.rem(self.at.x + step, 4)]
+            self.sent.append(self.go.remote(src, self.dx.at[n], self.at.at_x(step)))
+
+    def sixth(self):
+        for copy in self.sent:
+            copy.wait_recv()
+        self.ey[...] = add(self.ex[self.at.x], *[self.dx[n] for n in range(3)]).astype(BF16)
+        self.sent = []
+        for n, step in enumerate((2, 1, 3)):
+            src = self.ey.at[:, lanes(lax.rem(self.at.y + step, 4) * 128, 128)]
+            self.sent.append(self.go.remote(src, self.dy.at[n], self.at.at_y(step)))
+
+    def last(self):
+        for copy in self.sent:
+            copy.wait_recv()
+        return add(self.ey[:, lanes(self.at.y * 128, 128)], *[self.dy[n] for n in range(3)])
+
+
+Z_SCRATCH = (
+    pltpu.VMEM((2, 2, 32, 512), BF16),
+    pltpu.VMEM((2, 4, 32, 512), BF16),
+    pltpu.VMEM((2, 4, 32, 512), BF16),
+    pltpu.VMEM((2, 4, 32, 512), BF16),
+    pltpu.VMEM((4, 32, 512), BF16),
+    pltpu.VMEM((3, 32, 512), BF16),
+    pltpu.VMEM((32, 512), BF16),
+    pltpu.VMEM((3, 32, 128), BF16),
+)
+
+
 def pack_reduce(a, b, low):
     cut = slice(128 * low, 128 * low + 128)
     return jnp.concatenate([a[:, cut], b[:, cut]], 0)
@@ -387,7 +458,7 @@
     ]
 
 
-COPIES = 12 + 18 + 3 * 11 + 15 + 8 + 2 * (8 + 6 + 7) + 16
+COPIES = 12 + 18 + 3 * 11 + 15 + 8 + 2 * (8 + 6 + 7) + 14 + 16
 
 
 def block_kernel(
@@ -399,7 +470,7 @@
     blk, land, back, oland, ocland, wq, wo, wr,
     x_tok, cot_tok, qkv, qs, kh, rq, rk, probs, bias, bias_rows, table, mask, att, d_att, dqs, dkh, dqkv,
     xhat, xscale, ro, dproj, dtok, xt, at_t, ls_row, ro_cols, ro_theirs, x_cols, x_theirs, at_cols, at_theirs,
-    dred, dred_theirs, dproj_theirs, dqkv_theirs, fa, fb, mb,
+    dred, dred_theirs, dproj_theirs, dqkv_theirs, fa, fz, fb, mb,
     *rest,
     ) = rest
     held, rest = rest[:24], rest[24:]
@@ -409,7 +480,7 @@
         ng_ref, mg_ref, t_merge_ref, t_cmerge_ref, t_unblock_ref, t_unmerge_ref, t_cunblock_ref, t_cunmerge_ref,
         columns_ref, columns_16_ref, bd64_ref, bd32_ref, heads_ref,
     ) = held
-    a_bufs, b_bufs, (send_sem, recv_sem, local_sem) = rest[0:10], rest[10:20], rest[20:]
+    a_bufs, b_bufs, z_bufs, (send_sem, recv_sem, local_sem) = rest[0:10], rest[10:20], rest[20:28], rest[28:]
     go = Sender(send_sem, recv_sem, local_sem)
     at = Place()
     c = at.core
@@ -619,17 +690,25 @@
         copy.wait_recv()
     before_a = go.count
     a_sum = Reduce(at, go, fa, *a_bufs)
+    z_sum = ReduceZ(at, go, fz, *z_bufs)
     grads = jnp.concatenate([dred[...], dred_theirs[...]], 0)
     for n in range(4):
         k = a_sum.xs[n]
         rows = pl.ds(pl.multiple_of(64 * k, 64), 64)
         tokens = jnp.concatenate([ro_cols[rows, mine], ro_theirs[rows]], 0).T
-        for cut in (slice(0, 512), slice(512, 1024)):
+        for h in range(2):
+            cut = slice(512 * h, 512 * h + 512)
             got = mm(tokens, grads[:, cut]).astype(BF16).reshape(4, 64, 512)
-            fa[0, k, :, :, cut] = got[:, 0:32]
-            fa[1, k, :, :, cut] = got[:, 32:64]
+            fa[0, k, :, :, cut] = got[:, 0:16]
+            fa[1, k, :, :, cut] = got[:, 16:32]
+            for low in range(2):
+                for y in range(2):
+                    start = 256 * y + 128 * low
+                    to = slice(256 * h + 128 * y, 256 * h + 128 * y + 128)
+                    fz[:, low, k, :, to] = got[:, 32:64, start : start + 128]
         if n == 0:
             a_sum.first_x()
+    z_sum.first()
     a_sum.first_y()
 
     def backward(g):
@@ -657,6 +736,7 @@
     dqkv_swap = [swap_dqkv(1024)]
     a_sum.second_x()
     a_sum.second_y()
+    z_sum.step(1)
     for start, inverse, grad in ((0, rq, dqs), (512, rk, dkh)):
         for n in range(2):
             cut = slice(256 * n, 256 * n + 256)
@@ -686,6 +766,7 @@
     back[...] = mm(t_unmerge_ref[...], d_in.astype(BF16)).astype(BF16)
     grad_back = send_back(back, oland)
 
+    z_sum.step(2)
     for copy in dqkv_swap:
         copy.wait_recv()
     before_b = go.count
@@ -702,13 +783,16 @@
     go.drain(before_a // 2)
     a_sum.third_x()
     a_sum.third_y()
+    z_sum.step(3)
     b_sum.second_y()
     b_sum.second_x()
     go.drain(before_b)
     before_c = go.count
     a_sum.fourth(pack_reduce)
+    z_sum.fifth()
     b_sum.third_y()
     b_sum.third_x()
+    z_sum.sixth()
     b_sum.fourth(pack_qkv_out)
     go.drain(before_c)
     for copy in merged_back + grad_back:
@@ -720,7 +804,8 @@
     for q in range(4):
         merged_ref[:, :, 256 * q : 256 * q + 256] = got[64 * q : 64 * q + 64].reshape(4, 16, 256)
     factor = 1.0 / 256.0
-    gr_ref[...] = a_sum.fifth() * factor
+    gr_ref[0:32] = a_sum.fifth() * factor
+    gr_ref[32:64] = z_sum.last() * factor
     go.drain()
     total = b_sum.fifth() * factor
     gq_ref[:, 0:128] = total[0:16]
@@ -780,12 +865,14 @@
             pltpu.VMEM((64, 1024), BF16),
             pltpu.VMEM((64, 1024), BF16),
             tokens(512), tokens(1536),
-            pltpu.VMEM((2, 4, 4, 32, 1024), BF16),
+            pltpu.VMEM((2, 4, 4, 16, 1024), BF16),
+            pltpu.VMEM((4, 2, 4, 32, 512), BF16),
             pltpu.VMEM((2, 4, 4, 16, 1024), BF16),
             tokens(256),
             *[pltpu.VMEM(load.shape, load.dtype) for load in loads],
-            *reduce_scratch(32, 64),
             *reduce_scratch(16, 32),
+            *reduce_scratch(16, 32),
+            *Z_SCRATCH,
             sems((COPIES,)),
             sems((COPIES,)),
             sems((32,)),

time: 79.3 us -> 79.7 us (level)
  no operation moved by 1% of the time
where the time goes in v4:
time: 79.7 us; the launch traced here: 79.5 us
  Pallas kernels  78.9 us (99%)
    pallas_call x1, Pallas kernels, on_device(): pl.pallas_call(block_kernel, out_shape=outputs, in_specs=[pl.BlockSpec(me...  77.1 us
    pallas_call x1, Pallas kernels, on_device(): pl.pallas_call(hand_on, out_shape=outputs, in_specs=[vmem] * 5, out_specs...  1.78 us

profile of v4, /device:TPU:2, one launch (start us, length us, event | category | flops | bytes accessed | tf_op | source)
XLA Modules:
  0.0 79.5 jit_solution(2620471620138247456)
XLA Ops:
  0.6 77.1 %block_forward_backward.1 = (bf16[4,16,1024]{2,1,0:T(8,128)(2,1)}, bf16[8,32,512]{2,1,0:T(8,128)(2,1)}, f32[16,192]{1,0:T(8,128)}, f32[16,64]{1,0:T(8,128)}, f32[64,128]{1,0:T(8,128)}) custom-call(bf16[16,1536]{1,0:T(8,128)(2,1)} %wq_ref.1, bf16[16,512]{1,0:T(8,128)(2,1)} %wo_ref.1, bf16[64,1024]{1,0:T(8,128)(2,1)} %wr_ref.1, s32[8,32,512]{2,1,0:T(8,128)} %rest_0_.1, ...), custom_call_target="tpu_custom_call" | custom-call | tf_op jit(solution)/shard_map/block_forward_backward/pallas_call | solution.py:842
  77.7 1.8 %hand_on.1 = (bf16[4,16,1024]{2,1,0:T(8,128)(2,1)}, bf16[8,32,512]{2,1,0:T(8,128)(2,1)}, f32[16,192]{1,0:T(8,128)}, f32[16,64]{1,0:T(8,128)}, f32[64,128]{1,0:T(8,128)}) custom-call(bf16[4,16,1024]{2,1,0:T(8,128)(2,1)} %get-tuple-element.10.refs_0_, bf16[8,32,512]{2,1,0:T(8,128)(2,1)} %get-tuple-element.11.refs_1_, f32[16,192]{1,0:T(8,128)} %get-tuple-element.12.refs_2_, ...), custom_call_target="tpu_custom_call" | custom-call | tf_op jit(solution)/shard_map/hand_on/pallas_call | solution.py:885

commit v5 on v3

--- a/solution.py
+++ b/solution.py
@@ -264,7 +264,7 @@
 
 
 class Reduce:
-    def __init__(self, at, go, m, bx1, bx2, by1, by2, cx, cy, dx, dy, zsend, zland):
+    def __init__(self, at, go, m, bx1, bx2, by1, by2, cx, cy, dx, dy, zsend, zland, direct=False):
         self.at, self.go, self.m = at, go, m
         self.bx1, self.bx2, self.by1, self.by2 = bx1, bx2, by1, by2
         self.cx, self.cy = cx, cy
@@ -272,7 +272,8 @@
         self.zsend, self.zland = zsend, zland
         self.xs = [lax.rem(at.x + step, 4) for step in (2, 1, 3, 0)]
         self.ys = [lax.rem(at.y + step, 4) for step in (2, 1, 3, 0)]
-        self.d = []
+        self.direct, self.parts = direct, 3 if direct else 2
+        self.d, self.d_y = [], []
         self.x_left, self.x_right = at.at_x(-1), at.at_x(1)
         self.y_left, self.y_right = at.at_y(-1), at.at_y(1)
 
@@ -288,6 +289,14 @@
 
     def y_src(self, n, part):
         return self.m.at[1, part, :, :, y_cut(self.ys[n])]
+
+    def direct_y(self, n):
+        self.d_y = self.d_y + [self.go.remote(self.y_src(n, EVERY), self.by2.at[n], self.at.at_y((2, 1, 3)[n]))]
+
+    def direct_x(self):
+        self.d_x = [
+            self.go.remote(self.x_src(n, EVERY), self.bx2.at[n], self.at.at_x(step)) for n, step in ((0, 2), (1, 1), (2, 3))
+        ]
 
     def first_x(self):
         self.b_x = self.both(self.x_src, self.bx1, self.x_right, self.x_left, 1)
@@ -317,20 +326,21 @@
 
     def third_x(self):
         at = self.at
-        for copy in self.b_x:
+        for copy in self.d_x if self.direct else self.b_x:
             copy.wait_recv()
         for s in range(4):
-            self.cx[s] = add(self.m[0, at.x, s], self.bx2[0, s], self.bx2[1, s]).astype(BF16)
+            self.cx[s] = add(self.m[0, at.x, s], *[self.bx2[n, s] for n in range(self.parts)]).astype(BF16)
         for n, step in ((0, 2), (1, 1), (2, 3)):
             src = self.cx.at[:, :, y_cut(self.ys[n])]
             self.d.append(self.go.remote(src, self.dx.at[n], at.at_y(step)))
 
     def third_y(self):
         at = self.at
-        for copy in self.b_y:
+        for copy in self.d_y if self.direct else self.b_y:
             copy.wait_recv()
         for s in range(4):
-            self.cy[s] = add(self.m[1, s, :, :, y_cut(at.y)], self.by2[0, s], self.by2[1, s]).astype(BF16)
+            own = self.m[1, s, :, :, y_cut(at.y)]
+            self.cy[s] = add(own, *[self.by2[n, s] for n in range(self.parts)]).astype(BF16)
         for n, step in ((0, 2), (1, 1), (2, 3)):
             self.d.append(self.go.remote(self.cy.at[self.xs[n]], self.dy.at[n], at.at_x(step)))
 
@@ -372,12 +382,12 @@
     return jnp.concatenate(rows, 0)
 
 
-def reduce_scratch(rows, z_rows):
+def reduce_scratch(rows, z_rows, parts):
     return [
         pltpu.VMEM((2, 2, rows, 1024), BF16),
-        pltpu.VMEM((2, 4, rows, 1024), BF16),
+        pltpu.VMEM((parts, 4, rows, 1024), BF16),
         pltpu.VMEM((2, 2, 4, rows, 256), BF16),
-        pltpu.VMEM((2, 4, 4, rows, 256), BF16),
+        pltpu.VMEM((parts, 4, 4, rows, 256), BF16),
         pltpu.VMEM((4, rows, 1024), BF16),
         pltpu.VMEM((4, 4, rows, 256), BF16),
         pltpu.VMEM((3, 4, rows, 256), BF16),
@@ -689,7 +699,7 @@
     for copy in dqkv_swap:
         copy.wait_recv()
     before_b = go.count
-    b_sum = Reduce(at, go, fb, *b_bufs)
+    b_sum = Reduce(at, go, fb, *b_bufs, direct=True)
     for n in range(4):
         y = b_sum.ys[n]
         cut = lanes(384 * y, 384)
@@ -697,18 +707,17 @@
         got = mm(xt[...], grads).astype(BF16)
         fb[0, :, :, :, y_cut(y)] = got[:, 0:256].reshape(4, 4, 16, 256)
         fb[1, :, :, :, lanes(256 * y, 128)] = got[:, 256:384].reshape(4, 4, 16, 128)
-    b_sum.first_x()
-    b_sum.first_y()
+        if n < 3:
+            b_sum.direct_y(n)
+    b_sum.direct_x()
     go.drain(before_a // 2)
     a_sum.third_x()
     a_sum.third_y()
-    b_sum.second_y()
-    b_sum.second_x()
     go.drain(before_b)
     before_c = go.count
-    a_sum.fourth(pack_reduce)
     b_sum.third_y()
     b_sum.third_x()
+    a_sum.fourth(pack_reduce)
     b_sum.fourth(pack_qkv_out)
     go.drain(before_c)
     for copy in merged_back + grad_back:
@@ -784,8 +793,8 @@
             pltpu.VMEM((2, 4, 4, 16, 1024), BF16),
             tokens(256),
             *[pltpu.VMEM(load.shape, load.dtype) for load in loads],
-            *reduce_scratch(32, 64),
-            *reduce_scratch(16, 32),
+            *reduce_scratch(32, 64, 2),
+            *reduce_scratch(16, 32, 3),
             sems((COPIES,)),
             sems((COPIES,)),
             sems((32,)),

time: 79.3 us -> 77.7 us (0.980)
  Pallas kernels: 78.2 us -> 76.9 us
    pallas_call x1, Pallas kernels: 76.4 us -> 75.1 us  [on_device(): pl.pallas_call(block_kernel, out_shape=outputs, in_specs=[pl.BlockSpec(me...]
where the time goes in v5:
time: 77.7 us; the launch traced here: 77.5 us
  Pallas kernels  76.9 us (99%)
    pallas_call x1, Pallas kernels, on_device(): pl.pallas_call(block_kernel, out_shape=outputs, in_specs=[pl.BlockSpec(me...  75.1 us
    pallas_call x1, Pallas kernels, on_device(): pl.pallas_call(hand_on, out_shape=outputs, in_specs=[vmem] * 5, out_specs...  1.78 us

profile of v5, /device:TPU:2, one launch (start us, length us, event | category | flops | bytes accessed | tf_op | source)
XLA Modules:
  0.0 77.5 jit_solution(3769905890998218123)
XLA Ops:
  0.6 75.1 %block_forward_backward.1 = (bf16[4,16,1024]{2,1,0:T(8,128)(2,1)}, bf16[8,32,512]{2,1,0:T(8,128)(2,1)}, f32[16,192]{1,0:T(8,128)}, f32[16,64]{1,0:T(8,128)}, f32[64,128]{1,0:T(8,128)}) custom-call(bf16[16,1536]{1,0:T(8,128)(2,1)} %wq_ref.1, bf16[16,512]{1,0:T(8,128)(2,1)} %wo_ref.1, bf16[64,1024]{1,0:T(8,128)(2,1)} %wr_ref.1, s32[8,32,512]{2,1,0:T(8,128)} %rest_0_.1, ...), custom_call_target="tpu_custom_call" | custom-call | tf_op jit(solution)/shard_map/block_forward_backward/pallas_call | solution.py:766
  75.8 1.8 %hand_on.1 = (bf16[4,16,1024]{2,1,0:T(8,128)(2,1)}, bf16[8,32,512]{2,1,0:T(8,128)(2,1)}, f32[16,192]{1,0:T(8,128)}, f32[16,64]{1,0:T(8,128)}, f32[64,128]{1,0:T(8,128)}) custom-call(bf16[4,16,1024]{2,1,0:T(8,128)(2,1)} %get-tuple-element.10.refs_0_, bf16[8,32,512]{2,1,0:T(8,128)(2,1)} %get-tuple-element.11.refs_1_, f32[16,192]{1,0:T(8,128)} %get-tuple-element.12.refs_2_, ...), custom_call_target="tpu_custom_call" | custom-call | tf_op jit(solution)/shard_map/hand_on/pallas_call | solution.py:807

commit v6 on v3

--- a/solution.py
+++ b/solution.py
@@ -153,11 +153,8 @@
     return total
 
 
-def split_mm(values, table):
-    high = values.astype(BF16)
-    low = (values - high.astype(F32)).astype(BF16)
-    both = mm(jnp.concatenate([high, low], 0), table)
-    return both[: len(values)] + both[len(values) :]
+def sums(values, table):
+    return mm(values.astype(BF16), table)
 
 
 def norm_parts(values):
@@ -264,24 +261,15 @@
 
 
 class Reduce:
-    def __init__(self, at, go, m, bx1, bx2, by1, by2, cx, cy, dx, dy, zsend, zland):
+    def __init__(self, at, go, m, bx2, by2, cx, cy, dx, dy, zsend, zland):
         self.at, self.go, self.m = at, go, m
-        self.bx1, self.bx2, self.by1, self.by2 = bx1, bx2, by1, by2
+        self.bx2, self.by2 = bx2, by2
         self.cx, self.cy = cx, cy
         self.dx, self.dy = dx, dy
         self.zsend, self.zland = zsend, zland
         self.xs = [lax.rem(at.x + step, 4) for step in (2, 1, 3, 0)]
         self.ys = [lax.rem(at.y + step, 4) for step in (2, 1, 3, 0)]
-        self.d = []
-        self.x_left, self.x_right = at.at_x(-1), at.at_x(1)
-        self.y_left, self.y_right = at.at_y(-1), at.at_y(1)
-
-    def both(self, src, dst, right, left, step):
-        if step == 1:
-            pairs = ((src(0, pl.ds(0, 2)), right), (src(0, pl.ds(2, 2)), left))
-        else:
-            pairs = ((src(1, EVERY), right), (src(2, EVERY), left))
-        return [self.go.remote(ref, dst.at[n], device) for n, (ref, device) in enumerate(pairs)]
+        self.d, self.d_x, self.d_y = [], [], []
 
     def x_src(self, n, part):
         return self.m.at[0, self.xs[n], part]
@@ -289,48 +277,29 @@
     def y_src(self, n, part):
         return self.m.at[1, part, :, :, y_cut(self.ys[n])]
 
-    def first_x(self):
-        self.b_x = self.both(self.x_src, self.bx1, self.x_right, self.x_left, 1)
-
-    def first_y(self):
-        self.b_y = self.both(self.y_src, self.by1, self.y_right, self.y_left, 1)
-
-    def second_x(self):
-        m, xs = self.m, self.xs
-        for copy in self.b_x:
-            copy.wait_recv()
-        for s in range(2):
-            m[0, xs[1], s] = add(m[0, xs[1], s], self.bx1[0, s]).astype(BF16)
-            m[0, xs[2], 2 + s] = add(m[0, xs[2], 2 + s], self.bx1[1, s]).astype(BF16)
-        self.b_x = self.both(self.x_src, self.bx2, self.x_right, self.x_left, 2)
-
-    def second_y(self):
-        m, ys = self.m, self.ys
-        for copy in self.b_y:
-            copy.wait_recv()
-        for s in range(2):
-            cut = y_cut(ys[1])
-            m[1, s, :, :, cut] = add(m[1, s, :, :, cut], self.by1[0, s]).astype(BF16)
-            cut = y_cut(ys[2])
-            m[1, 2 + s, :, :, cut] = add(m[1, 2 + s, :, :, cut], self.by1[1, s]).astype(BF16)
-        self.b_y = self.both(self.y_src, self.by2, self.y_right, self.y_left, 2)
+    def direct_y(self, n):
+        self.d_y = self.d_y + [self.go.remote(self.y_src(n, EVERY), self.by2.at[n], self.at.at_y((2, 1, 3)[n]))]
+
+    def direct_x(self, n):
+        self.d_x = self.d_x + [self.go.remote(self.x_src(n, EVERY), self.bx2.at[n], self.at.at_x((2, 1, 3)[n]))]
 
     def third_x(self):
         at = self.at
-        for copy in self.b_x:
+        for copy in self.d_x:
             copy.wait_recv()
         for s in range(4):
-            self.cx[s] = add(self.m[0, at.x, s], self.bx2[0, s], self.bx2[1, s]).astype(BF16)
+            self.cx[s] = add(self.m[0, at.x, s], *[self.bx2[n, s] for n in range(3)]).astype(BF16)
         for n, step in ((0, 2), (1, 1), (2, 3)):
             src = self.cx.at[:, :, y_cut(self.ys[n])]
             self.d.append(self.go.remote(src, self.dx.at[n], at.at_y(step)))
 
     def third_y(self):
         at = self.at
-        for copy in self.b_y:
+        for copy in self.d_y:
             copy.wait_recv()
         for s in range(4):
-            self.cy[s] = add(self.m[1, s, :, :, y_cut(at.y)], self.by2[0, s], self.by2[1, s]).astype(BF16)
+            own = self.m[1, s, :, :, y_cut(at.y)]
+            self.cy[s] = add(own, *[self.by2[n, s] for n in range(3)]).astype(BF16)
         for n, step in ((0, 2), (1, 1), (2, 3)):
             self.d.append(self.go.remote(self.cy.at[self.xs[n]], self.dy.at[n], at.at_x(step)))
 
@@ -374,10 +343,8 @@
 
 def reduce_scratch(rows, z_rows):
     return [
-        pltpu.VMEM((2, 2, rows, 1024), BF16),
-        pltpu.VMEM((2, 4, rows, 1024), BF16),
-        pltpu.VMEM((2, 2, 4, rows, 256), BF16),
-        pltpu.VMEM((2, 4, 4, rows, 256), BF16),
+        pltpu.VMEM((3, 4, rows, 1024), BF16),
+        pltpu.VMEM((3, 4, 4, rows, 256), BF16),
         pltpu.VMEM((4, rows, 1024), BF16),
         pltpu.VMEM((4, 4, rows, 256), BF16),
         pltpu.VMEM((3, 4, rows, 256), BF16),
@@ -397,7 +364,7 @@
     (
     merged_ref, gin_ref, gq_ref, go_ref, gr_ref,
     blk, land, back, oland, ocland, wq, wo, wr,
-    x_tok, cot_tok, qkv, qs, kh, rq, rk, probs, bias, bias_rows, table, mask, att, d_att, dqs, dkh, dqkv,
+    x_tok, cot_tok, qkv, qs, kh, rq, rk, probs, masked, bias_rows, table, att, d_att, dqs, dkh, dqkv,
     xhat, xscale, ro, dproj, dtok, xt, at_t, ls_row, ro_cols, ro_theirs, x_cols, x_theirs, at_cols, at_theirs,
     dred, dred_theirs, dproj_theirs, dqkv_theirs, fa, fb, mb,
     *rest,
@@ -409,7 +376,7 @@
         ng_ref, mg_ref, t_merge_ref, t_cmerge_ref, t_unblock_ref, t_unmerge_ref, t_cunblock_ref, t_cunmerge_ref,
         columns_ref, columns_16_ref, bd64_ref, bd32_ref, heads_ref,
     ) = held
-    a_bufs, b_bufs, (send_sem, recv_sem, local_sem) = rest[0:10], rest[10:20], rest[20:]
+    a_bufs, b_bufs, (send_sem, recv_sem, local_sem) = rest[0:8], rest[8:16], rest[16:]
     go = Sender(send_sem, recv_sem, local_sem)
     at = Place()
     c = at.core
@@ -492,12 +459,14 @@
     q_y.y2()
     q_x.x3()
     o_x.x2()
-    for g in range(4):
-        bias[g] = jnp.concatenate([bias_rows[:, 4 * g + h, :] for h in range(4)], 1)
     last_rows = (at.wide == 31).astype(F32)
     last_cols = (at.narrow == 7).astype(F32)
-    mask[0] = row_cut_ref[...] * last_rows * -100.0
-    mask[1] = jnp.maximum(row_cut_ref[...] * last_rows, col_cut_ref[...] * last_cols) * -100.0
+    mask = row_cut_ref[...] * last_rows * -100.0
+    mask_end = jnp.maximum(row_cut_ref[...] * last_rows, col_cut_ref[...] * last_cols) * -100.0
+    for g in range(4):
+        bias = jnp.concatenate([bias_rows[:, 4 * g + h, :] for h in range(4)], 1)
+        masked[0, g] = bias + mask
+        masked[1, g] = bias + mask_end
     lane = lax.broadcasted_iota(jnp.int32, (1, 512), 1) // 32
     scales = jnp.zeros((1, 512), F32)
     for h in range(16):
@@ -534,7 +503,7 @@
             for row in range(0, 256, 128):
                 rows = slice(row, row + 128)
                 raw = qkv[rows, start + 256 * n : start + 256 * n + 256].astype(F32)
-                inv = lax.rsqrt(jnp.maximum(split_mm(raw * raw, bd32_ref[...]), 1e-24))
+                inv = lax.rsqrt(jnp.maximum(sums(raw * raw, bd32_ref[...]), 1e-24))
                 inverse[rows, cut] = inv
                 raw = raw * inv
                 if start == 0:
@@ -564,8 +533,8 @@
         weights = []
         for win in range(4):
             scores = dg(window(qs, win, cut), spread(window(kh, win, cut)), NT)
-            weights.append(jnp.exp(scores + bias[g] + mask[1 if win == 3 else 0]))
-        totals = split_mm(jnp.concatenate(weights, 0), bd64_ref[...])
+            weights.append(jnp.exp(scores + masked[1 if win == 3 else 0, g]))
+        totals = sums(jnp.concatenate(weights, 0), bd64_ref[...])
         for win in range(4):
             p = weights[win] / totals[64 * win : 64 * win + 64]
             probs[g, win] = p
@@ -628,9 +597,10 @@
             got = mm(tokens, grads[:, cut]).astype(BF16).reshape(4, 64, 512)
             fa[0, k, :, :, cut] = got[:, 0:32]
             fa[1, k, :, :, cut] = got[:, 32:64]
-        if n == 0:
-            a_sum.first_x()
-    a_sum.first_y()
+        if n < 3:
+            a_sum.direct_x(n)
+    for n in range(3):
+        a_sum.direct_y(n)
 
     def backward(g):
         cut = slice(g * 128, g * 128 + 128)
@@ -639,7 +609,7 @@
         for win in range(4):
             dp = dg(window(d_att, win, cut), spread(window(qkv, win, v_cut)), NT)
             dps.append(dp.astype(BF16).astype(F32))
-        alike = split_mm(jnp.concatenate([probs[g, win] * dps[win] for win in range(4)], 0), bd64_ref[...])
+        alike = sums(jnp.concatenate([probs[g, win] * dps[win] for win in range(4)], 0), bd64_ref[...])
         for win in range(4):
             p = probs[g, win]
             ds = (p * (dps[win] - alike[64 * win : 64 * win + 64])).astype(BF16)
@@ -655,8 +625,6 @@
         return go.remote(dqkv.at[:, cut], dqkv_theirs.at[:, cut], at.sibling)
 
     dqkv_swap = [swap_dqkv(1024)]
-    a_sum.second_x()
-    a_sum.second_y()
     for start, inverse, grad in ((0, rq, dqs), (512, rk, dkh)):
         for n in range(2):
             cut = slice(256 * n, 256 * n + 256)
@@ -668,7 +636,7 @@
                 d_unit = grad[rows, cut]
                 if start == 0:
                     d_unit = d_unit * ls_row[:, cut]
-                along = split_mm(unit * d_unit, bd32_ref[...])
+                along = sums(unit * d_unit, bd32_ref[...])
                 along = jnp.where(inv < 1e12, along, 0.0)
                 dqkv[rows, both_cut] = (inv * (d_unit - unit * along)).astype(BF16)
         dqkv_swap.append(swap_dqkv(start))
@@ -697,18 +665,18 @@
         got = mm(xt[...], grads).astype(BF16)
         fb[0, :, :, :, y_cut(y)] = got[:, 0:256].reshape(4, 4, 16, 256)
         fb[1, :, :, :, lanes(256 * y, 128)] = got[:, 256:384].reshape(4, 4, 16, 128)
-    b_sum.first_x()
-    b_sum.first_y()
+        if n < 3:
+            b_sum.direct_y(n)
+    for n in range(3):
+        b_sum.direct_x(n)
     go.drain(before_a // 2)
     a_sum.third_x()
     a_sum.third_y()
-    b_sum.second_y()
-    b_sum.second_x()
     go.drain(before_b)
     before_c = go.count
-    a_sum.fourth(pack_reduce)
     b_sum.third_y()
     b_sum.third_x()
+    a_sum.fourth(pack_reduce)
     b_sum.fourth(pack_qkv_out)
     go.drain(before_c)
     for copy in merged_back + grad_back:
@@ -768,10 +736,9 @@
             pltpu.VMEM((64, 1024), BF16),
             tokens(1536), tokens(512), tokens(512), tokens(512, F32), tokens(512, F32),
             pltpu.VMEM((4, 4, 64, 256), F32),
-            pltpu.VMEM((4, 64, 256), F32),
+            pltpu.VMEM((2, 4, 64, 256), F32),
             pltpu.VMEM((64, 16, 64), F32),
             pltpu.VMEM((16, 256), F32),
-            pltpu.VMEM((2, 64, 256), F32),
             tokens(512), tokens(512), tokens(512, F32), tokens(512, F32), tokens(1536),
             tokens(512, F32), tokens(1, F32), tokens(512), tokens(512), tokens(512),
             tokens(512), tokens(512),

time: 79.3 us -> 78.7 us (level)
  Pallas kernels: 78.2 us -> 77.1 us
    pallas_call x1, Pallas kernels: 76.4 us -> 75.3 us  [on_device(): pl.pallas_call(block_kernel, out_shape=outputs, in_specs=[pl.BlockSpec(me...]
where the time goes in v6:
time: 78.7 us; the launch traced here: 77.7 us
  Pallas kernels  77.1 us (98%)
    pallas_call x1, Pallas kernels, on_device(): pl.pallas_call(block_kernel, out_shape=outputs, in_specs=[pl.BlockSpec(me...  75.3 us
    pallas_call x1, Pallas kernels, on_device(): pl.pallas_call(hand_on, out_shape=outputs, in_specs=[vmem] * 5, out_specs...  1.78 us

profile of v6, /device:TPU:2, one launch (start us, length us, event | category | flops | bytes accessed | tf_op | source)
XLA Modules:
  0.0 77.7 jit_solution(4081964752674142704)
XLA Ops:
  0.6 75.3 %block_forward_backward.1 = (bf16[4,16,1024]{2,1,0:T(8,128)(2,1)}, bf16[8,32,512]{2,1,0:T(8,128)(2,1)}, f32[16,192]{1,0:T(8,128)}, f32[16,64]{1,0:T(8,128)}, f32[64,128]{1,0:T(8,128)}) custom-call(bf16[16,1536]{1,0:T(8,128)(2,1)} %wq_ref.1, bf16[16,512]{1,0:T(8,128)(2,1)} %wo_ref.1, bf16[64,1024]{1,0:T(8,128)(2,1)} %wr_ref.1, s32[8,32,512]{2,1,0:T(8,128)} %rest_0_.1, ...), custom_call_target="tpu_custom_call" | custom-call | tf_op jit(solution)/shard_map/block_forward_backward/pallas_call | solution.py:725
  75.9 1.8 %hand_on.1 = (bf16[4,16,1024]{2,1,0:T(8,128)(2,1)}, bf16[8,32,512]{2,1,0:T(8,128)(2,1)}, f32[16,192]{1,0:T(8,128)}, f32[16,64]{1,0:T(8,128)}, f32[64,128]{1,0:T(8,128)}) custom-call(bf16[4,16,1024]{2,1,0:T(8,128)(2,1)} %get-tuple-element.10.refs_0_, bf16[8,32,512]{2,1,0:T(8,128)(2,1)} %get-tuple-element.11.refs_1_, f32[16,192]{1,0:T(8,128)} %get-tuple-element.12.refs_2_, ...), custom_call_target="tpu_custom_call" | custom-call | tf_op jit(solution)/shard_map/hand_on/pallas_call | solution.py:765

commit v7 on v5

--- a/solution.py
+++ b/solution.py
@@ -77,6 +77,8 @@
         self.zl = lax.rem(narrow, 2)
         self.z = 2 * self.zh + self.zl
         self.sibling = (wide + 1 - 2 * self.core, narrow)
+        beside = narrow + 1 - 2 * self.zl
+        self.others = (self.sibling, (wide, beside), (self.sibling[0], beside))
 
     def at_x(self, step):
         return ((lax.rem(self.x + step + 4, 4) * 4 + self.zh) * 2 + self.core, self.narrow)
@@ -153,11 +155,8 @@
     return total
 
 
-def split_mm(values, table):
-    high = values.astype(BF16)
-    low = (values - high.astype(F32)).astype(BF16)
-    both = mm(jnp.concatenate([high, low], 0), table)
-    return both[: len(values)] + both[len(values) :]
+def sums(values, table):
+    return mm(values.astype(BF16), table)
 
 
 def norm_parts(values):
@@ -259,17 +258,14 @@
             copy.wait_recv()
 
 
-def y_cut(j):
-    return lanes(j * 256, 256)
-
-
 class Reduce:
-    def __init__(self, at, go, m, bx1, bx2, by1, by2, cx, cy, dx, dy, zsend, zland, direct=False):
+    def __init__(self, at, go, m, bx1, bx2, by1, by2, cx, cy, dx, dy, zsend, zland, width, z_steps, direct=False):
         self.at, self.go, self.m = at, go, m
         self.bx1, self.bx2, self.by1, self.by2 = bx1, bx2, by1, by2
         self.cx, self.cy = cx, cy
         self.dx, self.dy = dx, dy
         self.zsend, self.zland = zsend, zland
+        self.width, self.z_steps = width, z_steps
         self.xs = [lax.rem(at.x + step, 4) for step in (2, 1, 3, 0)]
         self.ys = [lax.rem(at.y + step, 4) for step in (2, 1, 3, 0)]
         self.direct, self.parts = direct, 3 if direct else 2
@@ -284,11 +280,14 @@
             pairs = ((src(1, EVERY), right), (src(2, EVERY), left))
         return [self.go.remote(ref, dst.at[n], device) for n, (ref, device) in enumerate(pairs)]
 
+    def y_cut(self, j):
+        return lanes(j * self.width, self.width)
+
     def x_src(self, n, part):
         return self.m.at[0, self.xs[n], part]
 
     def y_src(self, n, part):
-        return self.m.at[1, part, :, :, y_cut(self.ys[n])]
+        return self.m.at[1, part, :, :, self.y_cut(self.ys[n])]
 
     def direct_y(self, n):
         self.d_y = self.d_y + [self.go.remote(self.y_src(n, EVERY), self.by2.at[n], self.at.at_y((2, 1, 3)[n]))]
@@ -318,9 +317,9 @@
         for copy in self.b_y:
             copy.wait_recv()
         for s in range(2):
-            cut = y_cut(ys[1])
+            cut = self.y_cut(ys[1])
             m[1, s, :, :, cut] = add(m[1, s, :, :, cut], self.by1[0, s]).astype(BF16)
-            cut = y_cut(ys[2])
+            cut = self.y_cut(ys[2])
             m[1, 2 + s, :, :, cut] = add(m[1, 2 + s, :, :, cut], self.by1[1, s]).astype(BF16)
         self.b_y = self.both(self.y_src, self.by2, self.y_right, self.y_left, 2)
 
@@ -331,7 +330,7 @@
         for s in range(4):
             self.cx[s] = add(self.m[0, at.x, s], *[self.bx2[n, s] for n in range(self.parts)]).astype(BF16)
         for n, step in ((0, 2), (1, 1), (2, 3)):
-            src = self.cx.at[:, :, y_cut(self.ys[n])]
+            src = self.cx.at[:, :, self.y_cut(self.ys[n])]
             self.d.append(self.go.remote(src, self.dx.at[n], at.at_y(step)))
 
     def third_y(self):
@@ -339,36 +338,38 @@
         for copy in self.d_y if self.direct else self.b_y:
             copy.wait_recv()
         for s in range(4):
-            own = self.m[1, s, :, :, y_cut(at.y)]
+            own = self.m[1, s, :, :, self.y_cut(at.y)]
             self.cy[s] = add(own, *[self.by2[n, s] for n in range(self.parts)]).astype(BF16)
         for n, step in ((0, 2), (1, 1), (2, 3)):
             self.d.append(self.go.remote(self.cy.at[self.xs[n]], self.dy.at[n], at.at_x(step)))
 
+    def z_slot(self, step):
+        z = lax.rem(self.at.z + step, 8)
+        return lax.div(z, 2), lax.rem(z, 2) if len(self.z_steps) == 7 else 0
+
     def fourth(self, pack):
         for copy in self.d:
             copy.wait_recv()
         for h in range(4):
-            a = add(self.cx[h, :, y_cut(self.at.y)], *[self.dx[n, h] for n in range(3)])
+            a = add(self.cx[h, :, self.y_cut(self.at.y)], *[self.dx[n, h] for n in range(3)])
             b = add(self.cy[self.at.x, h], *[self.dy[n, h] for n in range(3)])
             for low in range(2):
-                self.zsend[h, low] = pack(a, b, low).astype(BF16)
+                if low == 0 or len(self.z_steps) == 7:
+                    self.zsend[h, low] = pack(a, b, low).astype(BF16)
         self.last = []
-        for step in range(1, 8):
-            z = lax.rem(self.at.z + step, 8)
-            src = self.zsend.at[lax.div(z, 2), lax.rem(z, 2)]
-            self.last.append(self.go.remote(src, self.zland.at[step - 1], self.at.at_z(step)))
+        for n, step in enumerate(self.z_steps):
+            self.last.append(self.go.remote(self.zsend.at[self.z_slot(step)], self.zland.at[n], self.at.at_z(step)))
 
     def fifth(self):
-        total = self.zsend[self.at.zh, self.at.zl].astype(F32)
-        for step in range(7):
-            self.last[step].wait_recv()
-            total = total + self.zland[step].astype(F32)
+        total = self.zsend[self.z_slot(0)].astype(F32)
+        for n, copy in enumerate(self.last):
+            copy.wait_recv()
+            total = total + self.zland[n].astype(F32)
         return total
 
 
 def pack_reduce(a, b, low):
-    cut = slice(128 * low, 128 * low + 128)
-    return jnp.concatenate([a[:, cut], b[:, cut]], 0)
+    return jnp.concatenate([a, b], 0)
 
 
 def pack_qkv_out(a, b, low):
@@ -382,16 +383,16 @@
     return jnp.concatenate(rows, 0)
 
 
-def reduce_scratch(rows, z_rows, parts):
+def reduce_scratch(rows, z_rows, parts, width):
     return [
-        pltpu.VMEM((2, 2, rows, 1024), BF16),
-        pltpu.VMEM((parts, 4, rows, 1024), BF16),
-        pltpu.VMEM((2, 2, 4, rows, 256), BF16),
-        pltpu.VMEM((parts, 4, 4, rows, 256), BF16),
-        pltpu.VMEM((4, rows, 1024), BF16),
-        pltpu.VMEM((4, 4, rows, 256), BF16),
-        pltpu.VMEM((3, 4, rows, 256), BF16),
-        pltpu.VMEM((3, 4, rows, 256), BF16),
+        pltpu.VMEM((2, 2, rows, 4 * width), BF16),
+        pltpu.VMEM((parts, 4, rows, 4 * width), BF16),
+        pltpu.VMEM((2, 2, 4, rows, width), BF16),
+        pltpu.VMEM((parts, 4, 4, rows, width), BF16),
+        pltpu.VMEM((4, rows, 4 * width), BF16),
+        pltpu.VMEM((4, 4, rows, width), BF16),
+        pltpu.VMEM((3, 4, rows, width), BF16),
+        pltpu.VMEM((3, 4, rows, width), BF16),
         pltpu.VMEM((4, 2, z_rows, 128), BF16),
         pltpu.VMEM((7, z_rows, 128), BF16),
     ]
@@ -407,9 +408,9 @@
     (
     merged_ref, gin_ref, gq_ref, go_ref, gr_ref,
     blk, land, back, oland, ocland, wq, wo, wr,
-    x_tok, cot_tok, qkv, qs, kh, rq, rk, probs, bias, bias_rows, table, mask, att, d_att, dqs, dkh, dqkv,
+    x_tok, cot_tok, qkv, qs, kh, rq, rk, probs, masked, bias_rows, table, att, d_att, dqs, dkh, dqkv,
     xhat, xscale, ro, dproj, dtok, xt, at_t, ls_row, ro_cols, ro_theirs, x_cols, x_theirs, at_cols, at_theirs,
-    dred, dred_theirs, dproj_theirs, dqkv_theirs, fa, fb, mb,
+    dred, dred_cols, dred_theirs, dproj_theirs, dqkv_theirs, fa, fb, mb,
     *rest,
     ) = rest
     held, rest = rest[:24], rest[24:]
@@ -424,7 +425,7 @@
     at = Place()
     c = at.core
     partners = (
-        [at.sibling]
+        [at.sibling, at.others[2]]
         + [at.at_x(step) for step in (1, 2, 3)]
         + [at.at_y(step) for step in (1, 2, 3)]
         + [at.at_z(step) for step in range(1, 8)]
@@ -502,12 +503,14 @@
     q_y.y2()
     q_x.x3()
     o_x.x2()
-    for g in range(4):
-        bias[g] = jnp.concatenate([bias_rows[:, 4 * g + h, :] for h in range(4)], 1)
     last_rows = (at.wide == 31).astype(F32)
     last_cols = (at.narrow == 7).astype(F32)
-    mask[0] = row_cut_ref[...] * last_rows * -100.0
-    mask[1] = jnp.maximum(row_cut_ref[...] * last_rows, col_cut_ref[...] * last_cols) * -100.0
+    mask = row_cut_ref[...] * last_rows * -100.0
+    mask_end = jnp.maximum(row_cut_ref[...] * last_rows, col_cut_ref[...] * last_cols) * -100.0
+    for g in range(4):
+        bias = jnp.concatenate([bias_rows[:, 4 * g + h, :] for h in range(4)], 1)
+        masked[0, g] = bias + mask
+        masked[1, g] = bias + mask_end
     lane = lax.broadcasted_iota(jnp.int32, (1, 512), 1) // 32
     scales = jnp.zeros((1, 512), F32)
     for h in range(16):
@@ -544,7 +547,7 @@
             for row in range(0, 256, 128):
                 rows = slice(row, row + 128)
                 raw = qkv[rows, start + 256 * n : start + 256 * n + 256].astype(F32)
-                inv = lax.rsqrt(jnp.maximum(split_mm(raw * raw, bd32_ref[...]), 1e-24))
+                inv = lax.rsqrt(jnp.maximum(sums(raw * raw, bd32_ref[...]), 1e-24))
                 inverse[rows, cut] = inv
                 raw = raw * inv
                 if start == 0:
@@ -574,8 +577,8 @@
         weights = []
         for win in range(4):
             scores = dg(window(qs, win, cut), spread(window(kh, win, cut)), NT)
-            weights.append(jnp.exp(scores + bias[g] + mask[1 if win == 3 else 0]))
-        totals = split_mm(jnp.concatenate(weights, 0), bd64_ref[...])
+            weights.append(jnp.exp(scores + masked[1 if win == 3 else 0, g]))
+        totals = sums(jnp.concatenate(weights, 0), bd64_ref[...])
         for win in range(4):
             p = weights[win] / totals[64 * win : 64 * win + 64]
             probs[g, win] = p
@@ -595,7 +598,10 @@
         xscale[rows] = scale
         ro[rows] = (x_tok[rows].astype(F32) + normed * ng_ref[...]).astype(BF16)
     ro_cols[...] = mm(ro[...], columns_ref[...]).astype(BF16)
-    swap = [go.remote(ro_cols.at[:, not_mine], ro_theirs, at.sibling)]
+    swap = [
+        go.remote(ro_cols.at[:, cut], ro_theirs.at[n], device)
+        for n, (device, cut) in enumerate(zip(at.others, (not_mine, mine, not_mine)))
+    ]
     r_x.done()
 
     reduced = jnp.zeros((64, 1024), F32)
@@ -603,7 +609,13 @@
         reduced += mm(ro[64 * k : 64 * k + 64], wr[k].reshape(512, 1024))
     normed, scale = norm_parts(reduced)
     dred[...] = norm_back(cot_tok[...].astype(F32), normed, scale, mg_ref[...]).astype(BF16)
-    swap.append(go.remote(dred, dred_theirs, at.sibling))
+    for low in range(2):
+        for y in range(4):
+            to, cut = slice(512 * low + 128 * y, 512 * low + 128 * y + 128), slice(256 * y + 128 * low, 256 * y + 128 * low + 128)
+            dred_cols[:, to] = dred[:, cut]
+    here, there = lanes(512 * at.zl, 512), lanes(512 * (1 - at.zl), 512)
+    for n, (device, cut) in enumerate(zip(at.others, (here, there, there))):
+        swap.append(go.remote(dred_cols.at[:, cut], dred_theirs.at[n], device))
     merged = (normed * mg_ref[...]).astype(BF16)
     merged = jnp.concatenate([merged[:, 256 * q : 256 * q + 256] for q in range(4)], 0)
     mb[...] = mm(t_cunmerge_ref[...], merged).astype(BF16)
@@ -628,16 +640,15 @@
     for copy in swap:
         copy.wait_recv()
     before_a = go.count
-    a_sum = Reduce(at, go, fa, *a_bufs)
-    grads = jnp.concatenate([dred[...], dred_theirs[...]], 0)
+    a_sum = Reduce(at, go, fa, *a_bufs, 128, (2, 4, 6))
+    grads = jnp.concatenate([dred_cols[:, here]] + [dred_theirs[n] for n in range(3)], 0)
     for n in range(4):
         k = a_sum.xs[n]
         rows = pl.ds(pl.multiple_of(64 * k, 64), 64)
-        tokens = jnp.concatenate([ro_cols[rows, mine], ro_theirs[rows]], 0).T
-        for cut in (slice(0, 512), slice(512, 1024)):
-            got = mm(tokens, grads[:, cut]).astype(BF16).reshape(4, 64, 512)
-            fa[0, k, :, :, cut] = got[:, 0:32]
-            fa[1, k, :, :, cut] = got[:, 32:64]
+        tokens = jnp.concatenate([ro_cols[rows, mine]] + [ro_theirs[m, rows] for m in range(3)], 0).T
+        got = mm(tokens, grads).astype(BF16).reshape(4, 64, 512)
+        fa[0, k] = got[:, 0:32]
+        fa[1, k] = got[:, 32:64]
         if n == 0:
             a_sum.first_x()
     a_sum.first_y()
@@ -649,7 +660,7 @@
         for win in range(4):
             dp = dg(window(d_att, win, cut), spread(window(qkv, win, v_cut)), NT)
             dps.append(dp.astype(BF16).astype(F32))
-        alike = split_mm(jnp.concatenate([probs[g, win] * dps[win] for win in range(4)], 0), bd64_ref[...])
+        alike = sums(jnp.concatenate([probs[g, win] * dps[win] for win in range(4)], 0), bd64_ref[...])
         for win in range(4):
             p = probs[g, win]
             ds = (p * (dps[win] - alike[64 * win : 64 * win + 64])).astype(BF16)
@@ -678,7 +689,7 @@
                 d_unit = grad[rows, cut]
                 if start == 0:
                     d_unit = d_unit * ls_row[:, cut]
-                along = split_mm(unit * d_unit, bd32_ref[...])
+                along = sums(unit * d_unit, bd32_ref[...])
                 along = jnp.where(inv < 1e12, along, 0.0)
                 dqkv[rows, both_cut] = (inv * (d_unit - unit * along)).astype(BF16)
         dqkv_swap.append(swap_dqkv(start))
@@ -699,13 +710,13 @@
     for copy in dqkv_swap:
         copy.wait_recv()
     before_b = go.count
-    b_sum = Reduce(at, go, fb, *b_bufs, direct=True)
+    b_sum = Reduce(at, go, fb, *b_bufs, 256, tuple(range(1, 8)), direct=True)
     for n in range(4):
         y = b_sum.ys[n]
         cut = lanes(384 * y, 384)
         grads = jnp.concatenate([dqkv[:, cut], dqkv_theirs[:, cut]], 0)
         got = mm(xt[...], grads).astype(BF16)
-        fb[0, :, :, :, y_cut(y)] = got[:, 0:256].reshape(4, 4, 16, 256)
+        fb[0, :, :, :, lanes(256 * y, 256)] = got[:, 0:256].reshape(4, 4, 16, 256)
         fb[1, :, :, :, lanes(256 * y, 128)] = got[:, 256:384].reshape(4, 4, 16, 128)
         if n < 3:
             b_sum.direct_y(n)
@@ -777,24 +788,26 @@
             pltpu.VMEM((64, 1024), BF16),
             tokens(1536), tokens(512), tokens(512), tokens(512, F32), tokens(512, F32),
             pltpu.VMEM((4, 4, 64, 256), F32),
-            pltpu.VMEM((4, 64, 256), F32),
+            pltpu.VMEM((2, 4, 64, 256), F32),
             pltpu.VMEM((64, 16, 64), F32),
             pltpu.VMEM((16, 256), F32),
-            pltpu.VMEM((2, 64, 256), F32),
             tokens(512), tokens(512), tokens(512, F32), tokens(512, F32), tokens(1536),
             tokens(512, F32), tokens(1, F32), tokens(512), tokens(512), tokens(512),
             tokens(512), tokens(512),
             pltpu.VMEM((1, 512), F32),
-            tokens(512), tokens(256), tokens(512), tokens(256), tokens(512), tokens(256),
+            tokens(512),
+            pltpu.VMEM((3, 256, 256), BF16),
+            tokens(512), tokens(256), tokens(512), tokens(256),
             pltpu.VMEM((64, 1024), BF16),
             pltpu.VMEM((64, 1024), BF16),
+            pltpu.VMEM((3, 64, 512), BF16),
             tokens(512), tokens(1536),
-            pltpu.VMEM((2, 4, 4, 32, 1024), BF16),
+            pltpu.VMEM((2, 4, 4, 32, 512), BF16),
             pltpu.VMEM((2, 4, 4, 16, 1024), BF16),
             tokens(256),
             *[pltpu.VMEM(load.shape, load.dtype) for load in loads],
-            *reduce_scratch(32, 64, 2),
-            *reduce_scratch(16, 32, 3),
+            *reduce_scratch(32, 64, 2, 128),
+            *reduce_scratch(16, 32, 3, 256),
             sems((COPIES,)),
             sems((COPIES,)),
             sems((32,)),

time: 77.7 us -> 78.3 us (level)
  no operation moved by 1% of the time
where the time goes in v7:
time: 78.3 us; the launch traced here: 78 us
  Pallas kernels  77.3 us (99%)
    pallas_call x1, Pallas kernels, on_device(): pl.pallas_call(block_kernel, out_shape=outputs, in_specs=[pl.BlockSpec(me...  75.5 us
    pallas_call x1, Pallas kernels, on_device(): pl.pallas_call(hand_on, out_shape=outputs, in_specs=[vmem] * 5, out_specs...  1.78 us

profile of v7, /device:TPU:2, one launch (start us, length us, event | category | flops | bytes accessed | tf_op | source)
XLA Modules:
  0.0 78.0 jit_solution(2143195220573891098)
XLA Ops:
  0.6 75.5 %block_forward_backward.1 = (bf16[4,16,1024]{2,1,0:T(8,128)(2,1)}, bf16[8,32,512]{2,1,0:T(8,128)(2,1)}, f32[16,192]{1,0:T(8,128)}, f32[16,64]{1,0:T(8,128)}, f32[64,128]{1,0:T(8,128)}) custom-call(bf16[16,1536]{1,0:T(8,128)(2,1)} %wq_ref.1, bf16[16,512]{1,0:T(8,128)(2,1)} %wo_ref.1, bf16[64,1024]{1,0:T(8,128)(2,1)} %wr_ref.1, s32[8,32,512]{2,1,0:T(8,128)} %rest_0_.1, ...), custom_call_target="tpu_custom_call" | custom-call | tf_op jit(solution)/shard_map/block_forward_backward/pallas_call | solution.py:777
  76.2 1.8 %hand_on.1 = (bf16[4,16,1024]{2,1,0:T(8,128)(2,1)}, bf16[8,32,512]{2,1,0:T(8,128)(2,1)}, f32[16,192]{1,0:T(8,128)}, f32[16,64]{1,0:T(8,128)}, f32[64,128]{1,0:T(8,128)}) custom-call(bf16[4,16,1024]{2,1,0:T(8,128)(2,1)} %get-tuple-element.10.refs_0_, bf16[8,32,512]{2,1,0:T(8,128)(2,1)} %get-tuple-element.11.refs_1_, f32[16,192]{1,0:T(8,128)} %get-tuple-element.12.refs_2_, ...), custom_call_target="tpu_custom_call" | custom-call | tf_op jit(solution)/shard_map/hand_on/pallas_call | solution.py:820

commit v8 on v5

--- a/solution.py
+++ b/solution.py
@@ -153,11 +153,8 @@
     return total
 
 
-def split_mm(values, table):
-    high = values.astype(BF16)
-    low = (values - high.astype(F32)).astype(BF16)
-    both = mm(jnp.concatenate([high, low], 0), table)
-    return both[: len(values)] + both[len(values) :]
+def sums(values, table):
+    return mm(values.astype(BF16), table)
 
 
 def norm_parts(values):
@@ -407,7 +404,7 @@
     (
     merged_ref, gin_ref, gq_ref, go_ref, gr_ref,
     blk, land, back, oland, ocland, wq, wo, wr,
-    x_tok, cot_tok, qkv, qs, kh, rq, rk, probs, bias, bias_rows, table, mask, att, d_att, dqs, dkh, dqkv,
+    x_tok, cot_tok, qkv, qs, kh, rq, rk, probs, masked, bias_rows, table, att, d_att, dqs, dkh, dqkv,
     xhat, xscale, ro, dproj, dtok, xt, at_t, ls_row, ro_cols, ro_theirs, x_cols, x_theirs, at_cols, at_theirs,
     dred, dred_theirs, dproj_theirs, dqkv_theirs, fa, fb, mb,
     *rest,
@@ -446,9 +443,30 @@
     r_y = Gather(at, go, wr_ref, wr, lambda y: (pl.ds(pl.multiple_of(16 * y, 16), 16), pl.ds(512, 512)), True, True)
 
     q_y.start()
+
+    def roll(cut):
+        return [
+            go.remote(blk.at[pl.ds(first, rows), cut], land.at[pl.ds(to, rows), cut], device)
+            for first, rows, to, device in (
+                (16, 112, 128, at.at_tile(-1, 0)),
+                (128, 16, 112, at.at_tile(0, -1)),
+                (0, 16, 240, at.at_tile(-1, -1)),
+            )
+        ]
+
+    loaded(0, 3)
+    factor_of = exp_ref[...]
+    factor_of = jnp.where(factor_of == -8, 2.0**-8, jnp.where(factor_of == -7, 2.0**-7, 2.0**-6))
+    in_window = lax.broadcasted_iota(jnp.int32, (32, 512), 0) // 8
+    factor = jnp.zeros((32, 512), F32)
+    for w in range(4):
+        factor = jnp.where(in_window == w, factor_of[:, w : w + 1], factor)
+    inputs = stash_ref[...].astype(F32) * factor[None]
+    blk[:, 0:512] = mm(t_block_ref[...], inputs.reshape(256, 512).astype(BF16)).astype(BF16)
+    halo = roll(pl.ds(0, 512))
     r_y.start()
 
-    loaded(0, 11)
+    loaded(3, 11)
     table[...] = jnp.zeros((16, 256), F32)
     table[:, 0:225] = 16.0 * jax.nn.sigmoid(table_ref[...])
     by_head = table[...]
@@ -471,29 +489,17 @@
     bias_of(range(0, 5))
     o_x.start()
 
-    factor_of = exp_ref[...]
-    factor_of = jnp.where(factor_of == -8, 2.0**-8, jnp.where(factor_of == -7, 2.0**-7, 2.0**-6))
-    in_window = lax.broadcasted_iota(jnp.int32, (32, 512), 0) // 8
-    factor = jnp.zeros((32, 512), F32)
-    for w in range(4):
-        factor = jnp.where(in_window == w, factor_of[:, w : w + 1], factor)
-    inputs = stash_ref[...].astype(F32) * factor[None]
-    blk[:, 0:512] = mm(t_block_ref[...], inputs.reshape(256, 512).astype(BF16)).astype(BF16)
     q_x.start()
     q_y.x1()
     cot = cot_ref[...].astype(F32).reshape(64, 1024).astype(BF16)
     cot = jnp.concatenate([cot[:, 256 * q : 256 * q + 256] for q in range(4)], 0)
     blk[:, 512:768] = mm(t_cblock_ref[...], cot).astype(BF16)
+    cot_halo = roll(pl.ds(512, 256))
     r_y.x1()
     r_x.start()
     q_x.x1()
     q_y.y1()
     o_x.x1()
-    halo = [
-        go.remote(blk.at[pl.ds(16, 112)], land.at[pl.ds(128, 112)], at.at_tile(-1, 0)),
-        go.remote(blk.at[pl.ds(128, 16)], land.at[pl.ds(112, 16)], at.at_tile(0, -1)),
-        go.remote(blk.at[pl.ds(0, 16)], land.at[pl.ds(240, 16)], at.at_tile(-1, -1)),
-    ]
     bias_of(range(5, 10))
     r_y.y1()
     q_x.x2()
@@ -502,12 +508,14 @@
     q_y.y2()
     q_x.x3()
     o_x.x2()
-    for g in range(4):
-        bias[g] = jnp.concatenate([bias_rows[:, 4 * g + h, :] for h in range(4)], 1)
     last_rows = (at.wide == 31).astype(F32)
     last_cols = (at.narrow == 7).astype(F32)
-    mask[0] = row_cut_ref[...] * last_rows * -100.0
-    mask[1] = jnp.maximum(row_cut_ref[...] * last_rows, col_cut_ref[...] * last_cols) * -100.0
+    mask = row_cut_ref[...] * last_rows * -100.0
+    mask_end = jnp.maximum(row_cut_ref[...] * last_rows, col_cut_ref[...] * last_cols) * -100.0
+    for g in range(4):
+        bias = jnp.concatenate([bias_rows[:, 4 * g + h, :] for h in range(4)], 1)
+        masked[0, g] = bias + mask
+        masked[1, g] = bias + mask_end
     lane = lax.broadcasted_iota(jnp.int32, (1, 512), 1) // 32
     scales = jnp.zeros((1, 512), F32)
     for h in range(16):
@@ -522,10 +530,8 @@
     r_x.x2()
     o_x.x3()
     loaded(11, 24)
-    land[pl.ds(0, 112)] = blk[pl.ds(144, 112)]
+    land[pl.ds(0, 112), 0:512] = blk[pl.ds(144, 112), 0:512]
     x_tok[...] = mm(t_merge_ref[...], land[:, 0:512]).astype(BF16)
-    cot = mm(t_cmerge_ref[...], land[:, 512:768]).astype(BF16)
-    cot_tok[...] = jnp.concatenate([cot[64 * q : 64 * q + 64] for q in range(4)], 1)
     x_cols[...] = mm(x_tok[...], columns_16_ref[...]).astype(BF16)
     not_mine = lanes(256 * (1 - c), 256)
     mine = lanes(256 * c, 256)
@@ -544,7 +550,7 @@
             for row in range(0, 256, 128):
                 rows = slice(row, row + 128)
                 raw = qkv[rows, start + 256 * n : start + 256 * n + 256].astype(F32)
-                inv = lax.rsqrt(jnp.maximum(split_mm(raw * raw, bd32_ref[...]), 1e-24))
+                inv = lax.rsqrt(jnp.maximum(sums(raw * raw, bd32_ref[...]), 1e-24))
                 inverse[rows, cut] = inv
                 raw = raw * inv
                 if start == 0:
@@ -574,8 +580,8 @@
         weights = []
         for win in range(4):
             scores = dg(window(qs, win, cut), spread(window(kh, win, cut)), NT)
-            weights.append(jnp.exp(scores + bias[g] + mask[1 if win == 3 else 0]))
-        totals = split_mm(jnp.concatenate(weights, 0), bd64_ref[...])
+            weights.append(jnp.exp(scores + masked[1 if win == 3 else 0, g]))
+        totals = sums(jnp.concatenate(weights, 0), bd64_ref[...])
         for win in range(4):
             p = weights[win] / totals[64 * win : 64 * win + 64]
             probs[g, win] = p
@@ -586,6 +592,11 @@
         forward(g)
     at_cols[...] = mm(att[...], columns_16_ref[...]).astype(BF16)
     at_swap = go.remote(at_cols.at[:, not_mine], at_theirs, at.sibling)
+    for copy in cot_halo:
+        copy.wait_recv()
+    land[pl.ds(0, 112), 512:768] = blk[pl.ds(144, 112), 512:768]
+    cot = mm(t_cmerge_ref[...], land[:, 512:768]).astype(BF16)
+    cot_tok[...] = jnp.concatenate([cot[64 * q : 64 * q + 64] for q in range(4)], 1)
     r_y.done()
     xhat[...] = mm(att[...], wo[...].reshape(512, 512))
     for row in range(0, 256, 64):
@@ -649,7 +660,7 @@
         for win in range(4):
             dp = dg(window(d_att, win, cut), spread(window(qkv, win, v_cut)), NT)
             dps.append(dp.astype(BF16).astype(F32))
-        alike = split_mm(jnp.concatenate([probs[g, win] * dps[win] for win in range(4)], 0), bd64_ref[...])
+        alike = sums(jnp.concatenate([probs[g, win] * dps[win] for win in range(4)], 0), bd64_ref[...])
         for win in range(4):
             p = probs[g, win]
             ds = (p * (dps[win] - alike[64 * win : 64 * win + 64])).astype(BF16)
@@ -678,7 +689,7 @@
                 d_unit = grad[rows, cut]
                 if start == 0:
                     d_unit = d_unit * ls_row[:, cut]
-                along = split_mm(unit * d_unit, bd32_ref[...])
+                along = sums(unit * d_unit, bd32_ref[...])
                 along = jnp.where(inv < 1e12, along, 0.0)
                 dqkv[rows, both_cut] = (inv * (d_unit - unit * along)).astype(BF16)
         dqkv_swap.append(swap_dqkv(start))
@@ -777,10 +788,9 @@
             pltpu.VMEM((64, 1024), BF16),
             tokens(1536), tokens(512), tokens(512), tokens(512, F32), tokens(512, F32),
             pltpu.VMEM((4, 4, 64, 256), F32),
-            pltpu.VMEM((4, 64, 256), F32),
+            pltpu.VMEM((2, 4, 64, 256), F32),
             pltpu.VMEM((64, 16, 64), F32),
             pltpu.VMEM((16, 256), F32),
-            pltpu.VMEM((2, 64, 256), F32),
             tokens(512), tokens(512), tokens(512, F32), tokens(512, F32), tokens(1536),
             tokens(512, F32), tokens(1, F32), tokens(512), tokens(512), tokens(512),
             tokens(512), tokens(512),

time: 77.7 us -> 81.4 us (1.048)
  Pallas kernels: 76.9 us -> 80.6 us
    pallas_call x1, Pallas kernels: 75.1 us -> 78.9 us  [on_device(): pl.pallas_call(block_kernel, out_shape=outputs, in_specs=[pl.BlockSpec(me...]
where the time goes in v8:
time: 81.4 us; the launch traced here: 81.3 us
  Pallas kernels  80.6 us (99%)
    pallas_call x1, Pallas kernels, on_device(): pl.pallas_call(block_kernel, out_shape=outputs, in_specs=[pl.BlockSpec(me...  78.9 us
    pallas_call x1, Pallas kernels, on_device(): pl.pallas_call(hand_on, out_shape=outputs, in_specs=[vmem] * 5, out_specs...  1.78 us

profile of v8, /device:TPU:2, one launch (start us, length us, event | category | flops | bytes accessed | tf_op | source)
XLA Modules:
  0.0 81.3 jit_solution(16542955397797573915)
XLA Ops:
  0.6 78.9 %block_forward_backward.1 = (bf16[4,16,1024]{2,1,0:T(8,128)(2,1)}, bf16[8,32,512]{2,1,0:T(8,128)(2,1)}, f32[16,192]{1,0:T(8,128)}, f32[16,64]{1,0:T(8,128)}, f32[64,128]{1,0:T(8,128)}) custom-call(bf16[16,1536]{1,0:T(8,128)(2,1)} %wq_ref.1, bf16[16,512]{1,0:T(8,128)(2,1)} %wo_ref.1, bf16[64,1024]{1,0:T(8,128)(2,1)} %wr_ref.1, s32[8,32,512]{2,1,0:T(8,128)} %rest_0_.1, ...), custom_call_target="tpu_custom_call" | custom-call | tf_op jit(solution)/shard_map/block_forward_backward/pallas_call | solution.py:777
  79.5 1.8 %hand_on.1 = (bf16[4,16,1024]{2,1,0:T(8,128)(2,1)}, bf16[8,32,512]{2,1,0:T(8,128)(2,1)}, f32[16,192]{1,0:T(8,128)}, f32[16,64]{1,0:T(8,128)}, f32[64,128]{1,0:T(8,128)}) custom-call(bf16[4,16,1024]{2,1,0:T(8,128)(2,1)} %get-tuple-element.10.refs_0_, bf16[8,32,512]{2,1,0:T(8,128)(2,1)} %get-tuple-element.11.refs_1_, f32[16,192]{1,0:T(8,128)} %get-tuple-element.12.refs_2_, ...), custom_call_target="tpu_custom_call" | custom-call | tf_op jit(solution)/shard_map/hand_on/pallas_call | solution.py:817

commit v9 on v5

--- a/solution.py
+++ b/solution.py
@@ -153,11 +153,8 @@
     return total
 
 
-def split_mm(values, table):
-    high = values.astype(BF16)
-    low = (values - high.astype(F32)).astype(BF16)
-    both = mm(jnp.concatenate([high, low], 0), table)
-    return both[: len(values)] + both[len(values) :]
+def sums(values, table):
+    return mm(values.astype(BF16), table)
 
 
 def norm_parts(values):
@@ -407,7 +404,7 @@
     (
     merged_ref, gin_ref, gq_ref, go_ref, gr_ref,
     blk, land, back, oland, ocland, wq, wo, wr,
-    x_tok, cot_tok, qkv, qs, kh, rq, rk, probs, bias, bias_rows, table, mask, att, d_att, dqs, dkh, dqkv,
+    x_tok, cot_tok, qkv, qs, kh, rq, rk, probs, masked, bias_rows, table, att, d_att, dqs, dkh, dqkv,
     xhat, xscale, ro, dproj, dtok, xt, at_t, ls_row, ro_cols, ro_theirs, x_cols, x_theirs, at_cols, at_theirs,
     dred, dred_theirs, dproj_theirs, dqkv_theirs, fa, fb, mb,
     *rest,
@@ -442,11 +439,11 @@
     q_y = Gather(at, go, wq_ref, wq, lambda y: (all_rows, lanes(512 + 256 * y, 256)), True, True)
     q_x = Gather(at, go, wq_ref, wq, lambda y: (all_rows, pl.ds(0, 512)))
     o_x = Gather(at, go, wo_ref, wo, lambda y: (all_rows, pl.ds(0, 512)))
-    r_x = Gather(at, go, wr_ref, wr, lambda y: (pl.ds(0, 64), pl.ds(0, 512)))
-    r_y = Gather(at, go, wr_ref, wr, lambda y: (pl.ds(pl.multiple_of(16 * y, 16), 16), pl.ds(512, 512)), True, True)
-
+    r_x = Gather(at, go, wr_ref, wr, lambda y: (pl.ds(0, 64), pl.ds(0, 640)))
+    r_y = Gather(at, go, wr_ref, wr, lambda y: (pl.ds(pl.multiple_of(16 * y, 16), 16), pl.ds(640, 384)), True, True)
+
+    r_y.start()
     q_y.start()
-    r_y.start()
 
     loaded(0, 11)
     table[...] = jnp.zeros((16, 256), F32)
@@ -480,11 +477,11 @@
     inputs = stash_ref[...].astype(F32) * factor[None]
     blk[:, 0:512] = mm(t_block_ref[...], inputs.reshape(256, 512).astype(BF16)).astype(BF16)
     q_x.start()
+    r_y.x1()
     q_y.x1()
     cot = cot_ref[...].astype(F32).reshape(64, 1024).astype(BF16)
     cot = jnp.concatenate([cot[:, 256 * q : 256 * q + 256] for q in range(4)], 0)
     blk[:, 512:768] = mm(t_cblock_ref[...], cot).astype(BF16)
-    r_y.x1()
     r_x.start()
     q_x.x1()
     q_y.y1()
@@ -502,12 +499,14 @@
     q_y.y2()
     q_x.x3()
     o_x.x2()
-    for g in range(4):
-        bias[g] = jnp.concatenate([bias_rows[:, 4 * g + h, :] for h in range(4)], 1)
     last_rows = (at.wide == 31).astype(F32)
     last_cols = (at.narrow == 7).astype(F32)
-    mask[0] = row_cut_ref[...] * last_rows * -100.0
-    mask[1] = jnp.maximum(row_cut_ref[...] * last_rows, col_cut_ref[...] * last_cols) * -100.0
+    mask = row_cut_ref[...] * last_rows * -100.0
+    mask_end = jnp.maximum(row_cut_ref[...] * last_rows, col_cut_ref[...] * last_cols) * -100.0
+    for g in range(4):
+        bias = jnp.concatenate([bias_rows[:, 4 * g + h, :] for h in range(4)], 1)
+        masked[0, g] = bias + mask
+        masked[1, g] = bias + mask_end
     lane = lax.broadcasted_iota(jnp.int32, (1, 512), 1) // 32
     scales = jnp.zeros((1, 512), F32)
     for h in range(16):
@@ -544,7 +543,7 @@
             for row in range(0, 256, 128):
                 rows = slice(row, row + 128)
                 raw = qkv[rows, start + 256 * n : start + 256 * n + 256].astype(F32)
-                inv = lax.rsqrt(jnp.maximum(split_mm(raw * raw, bd32_ref[...]), 1e-24))
+                inv = lax.rsqrt(jnp.maximum(sums(raw * raw, bd32_ref[...]), 1e-24))
                 inverse[rows, cut] = inv
                 raw = raw * inv
                 if start == 0:
@@ -574,8 +573,8 @@
         weights = []
         for win in range(4):
             scores = dg(window(qs, win, cut), spread(window(kh, win, cut)), NT)
-            weights.append(jnp.exp(scores + bias[g] + mask[1 if win == 3 else 0]))
-        totals = split_mm(jnp.concatenate(weights, 0), bd64_ref[...])
+            weights.append(jnp.exp(scores + masked[1 if win == 3 else 0, g]))
+        totals = sums(jnp.concatenate(weights, 0), bd64_ref[...])
         for win in range(4):
             p = weights[win] / totals[64 * win : 64 * win + 64]
             probs[g, win] = p
@@ -649,7 +648,7 @@
         for win in range(4):
             dp = dg(window(d_att, win, cut), spread(window(qkv, win, v_cut)), NT)
             dps.append(dp.astype(BF16).astype(F32))
-        alike = split_mm(jnp.concatenate([probs[g, win] * dps[win] for win in range(4)], 0), bd64_ref[...])
+        alike = sums(jnp.concatenate([probs[g, win] * dps[win] for win in range(4)], 0), bd64_ref[...])
         for win in range(4):
             p = probs[g, win]
             ds = (p * (dps[win] - alike[64 * win : 64 * win + 64])).astype(BF16)
@@ -678,7 +677,7 @@
                 d_unit = grad[rows, cut]
                 if start == 0:
                     d_unit = d_unit * ls_row[:, cut]
-                along = split_mm(unit * d_unit, bd32_ref[...])
+                along = sums(unit * d_unit, bd32_ref[...])
                 along = jnp.where(inv < 1e12, along, 0.0)
                 dqkv[rows, both_cut] = (inv * (d_unit - unit * along)).astype(BF16)
         dqkv_swap.append(swap_dqkv(start))
@@ -777,10 +776,9 @@
             pltpu.VMEM((64, 1024), BF16),
             tokens(1536), tokens(512), tokens(512), tokens(512, F32), tokens(512, F32),
             pltpu.VMEM((4, 4, 64, 256), F32),
-            pltpu.VMEM((4, 64, 256), F32),
+            pltpu.VMEM((2, 4, 64, 256), F32),
             pltpu.VMEM((64, 16, 64), F32),
             pltpu.VMEM((16, 256), F32),
-            pltpu.VMEM((2, 64, 256), F32),
             tokens(512), tokens(512), tokens(512, F32), tokens(512, F32), tokens(1536),
             tokens(512, F32), tokens(1, F32), tokens(512), tokens(512), tokens(512),
             tokens(512), tokens(512),

time: 77.7 us -> 79.9 us (1.028)
  Pallas kernels: 76.9 us -> 78.9 us
    pallas_call x1, Pallas kernels: 75.1 us -> 77.1 us  [on_device(): pl.pallas_call(block_kernel, out_shape=outputs, in_specs=[pl.BlockSpec(me...]
where the time goes in v9:
time: 79.9 us; the launch traced here: 79.6 us
  Pallas kernels  78.9 us (99%)
    pallas_call x1, Pallas kernels, on_device(): pl.pallas_call(block_kernel, out_shape=outputs, in_specs=[pl.BlockSpec(me...  77.1 us
    pallas_call x1, Pallas kernels, on_device(): pl.pallas_call(hand_on, out_shape=outputs, in_specs=[vmem] * 5, out_specs...  1.78 us

profile of v9, /device:TPU:2, one launch (start us, length us, event | category | flops | bytes accessed | tf_op | source)
XLA Modules:
  0.0 79.6 jit_solution(7756218833335037956)
XLA Ops:
  0.6 77.1 %block_forward_backward.1 = (bf16[4,16,1024]{2,1,0:T(8,128)(2,1)}, bf16[8,32,512]{2,1,0:T(8,128)(2,1)}, f32[16,192]{1,0:T(8,128)}, f32[16,64]{1,0:T(8,128)}, f32[64,128]{1,0:T(8,128)}) custom-call(bf16[16,1536]{1,0:T(8,128)(2,1)} %wq_ref.1, bf16[16,512]{1,0:T(8,128)(2,1)} %wo_ref.1, bf16[64,1024]{1,0:T(8,128)(2,1)} %wr_ref.1, s32[8,32,512]{2,1,0:T(8,128)} %rest_0_.1, ...), custom_call_target="tpu_custom_call" | custom-call | tf_op jit(solution)/shard_map/block_forward_backward/pallas_call | solution.py:765
  77.8 1.8 %hand_on.1 = (bf16[4,16,1024]{2,1,0:T(8,128)(2,1)}, bf16[8,32,512]{2,1,0:T(8,128)(2,1)}, f32[16,192]{1,0:T(8,128)}, f32[16,64]{1,0:T(8,128)}, f32[64,128]{1,0:T(8,128)}) custom-call(bf16[4,16,1024]{2,1,0:T(8,128)(2,1)} %get-tuple-element.10.refs_0_, bf16[8,32,512]{2,1,0:T(8,128)(2,1)} %get-tuple-element.11.refs_1_, f32[16,192]{1,0:T(8,128)} %get-tuple-element.12.refs_2_, ...), custom_call_target="tpu_custom_call" | custom-call | tf_op jit(solution)/shard_map/hand_on/pallas_call | solution.py:805

commit v10 on v9

--- a/solution.py
+++ b/solution.py
@@ -439,11 +439,11 @@
     q_y = Gather(at, go, wq_ref, wq, lambda y: (all_rows, lanes(512 + 256 * y, 256)), True, True)
     q_x = Gather(at, go, wq_ref, wq, lambda y: (all_rows, pl.ds(0, 512)))
     o_x = Gather(at, go, wo_ref, wo, lambda y: (all_rows, pl.ds(0, 512)))
-    r_x = Gather(at, go, wr_ref, wr, lambda y: (pl.ds(0, 64), pl.ds(0, 640)))
-    r_y = Gather(at, go, wr_ref, wr, lambda y: (pl.ds(pl.multiple_of(16 * y, 16), 16), pl.ds(640, 384)), True, True)
-
+    r_x = Gather(at, go, wr_ref, wr, lambda y: (pl.ds(0, 64), pl.ds(0, 512)))
+    r_y = Gather(at, go, wr_ref, wr, lambda y: (pl.ds(pl.multiple_of(16 * y, 16), 16), pl.ds(512, 512)), True, True)
+
+    q_y.start()
     r_y.start()
-    q_y.start()
 
     loaded(0, 11)
     table[...] = jnp.zeros((16, 256), F32)
@@ -477,11 +477,11 @@
     inputs = stash_ref[...].astype(F32) * factor[None]
     blk[:, 0:512] = mm(t_block_ref[...], inputs.reshape(256, 512).astype(BF16)).astype(BF16)
     q_x.start()
-    r_y.x1()
     q_y.x1()
     cot = cot_ref[...].astype(F32).reshape(64, 1024).astype(BF16)
     cot = jnp.concatenate([cot[:, 256 * q : 256 * q + 256] for q in range(4)], 0)
     blk[:, 512:768] = mm(t_cblock_ref[...], cot).astype(BF16)
+    r_y.x1()
     r_x.start()
     q_x.x1()
     q_y.y1()

time: 79.9 us -> 77.1 us (0.965)
  Pallas kernels: 78.9 us -> 76.4 us
    pallas_call x1, Pallas kernels: 77.1 us -> 74.6 us  [on_device(): pl.pallas_call(block_kernel, out_shape=outputs, in_specs=[pl.BlockSpec(me...]
where the time goes in v10:
time: 77.1 us; the launch traced here: 77 us
  Pallas kernels  76.4 us (99%)
    pallas_call x1, Pallas kernels, on_device(): pl.pallas_call(block_kernel, out_shape=outputs, in_specs=[pl.BlockSpec(me...  74.6 us
    pallas_call x1, Pallas kernels, on_device(): pl.pallas_call(hand_on, out_shape=outputs, in_specs=[vmem] * 5, out_specs...  1.78 us

profile of v10, /device:TPU:2, one launch (start us, length us, event | category | flops | bytes accessed | tf_op | source)
XLA Modules:
  0.0 77.0 jit_solution(13982718591657675503)
XLA Ops:
  0.6 74.6 %block_forward_backward.1 = (bf16[4,16,1024]{2,1,0:T(8,128)(2,1)}, bf16[8,32,512]{2,1,0:T(8,128)(2,1)}, f32[16,192]{1,0:T(8,128)}, f32[16,64]{1,0:T(8,128)}, f32[64,128]{1,0:T(8,128)}) custom-call(bf16[16,1536]{1,0:T(8,128)(2,1)} %wq_ref.1, bf16[16,512]{1,0:T(8,128)(2,1)} %wo_ref.1, bf16[64,1024]{1,0:T(8,128)(2,1)} %wr_ref.1, s32[8,32,512]{2,1,0:T(8,128)} %rest_0_.1, ...), custom_call_target="tpu_custom_call" | custom-call | tf_op jit(solution)/shard_map/block_forward_backward/pallas_call | solution.py:765
  75.2 1.8 %hand_on.1 = (bf16[4,16,1024]{2,1,0:T(8,128)(2,1)}, bf16[8,32,512]{2,1,0:T(8,128)(2,1)}, f32[16,192]{1,0:T(8,128)}, f32[16,64]{1,0:T(8,128)}, f32[64,128]{1,0:T(8,128)}) custom-call(bf16[4,16,1024]{2,1,0:T(8,128)(2,1)} %get-tuple-element.10.refs_0_, bf16[8,32,512]{2,1,0:T(8,128)(2,1)} %get-tuple-element.11.refs_1_, f32[16,192]{1,0:T(8,128)} %get-tuple-element.12.refs_2_, ...), custom_call_target="tpu_custom_call" | custom-call | tf_op jit(solution)/shard_map/hand_on/pallas_call | solution.py:805
